TPU v7x, 512 devices: a whole 4x8x8 slice. The times are simulated.
512 devices in a mesh: ctx: 64 (over z, y), resp: 8 (over x, core).
Axes of the slice: x: 4, y: 8, z: 8, core: 2. Of those that a mesh axis runs over, the one named last changes fastest.
Arguments:
- queries: bfloat16 [64, 128, 8192], P('resp', None, 'ctx'), may hold values from -70 to 70
- keys: bfloat16 [32768, 1024], P('ctx'), may hold values from -40.5 to 40.5
- values: bfloat16 [32768, 1024], P('ctx'), may hold values from -48 to 48
- span_ids: int32 [64, 2], P('resp'), may hold values from 0 to 15, all different within a row; in each aligned block of 8 rows (0 to 7, 8 to 15, ...) at most 2 rows name the same one
- lengths: int32 [64], P('resp'), may hold values from 1 to 2
- judge: float32 [8192], replicated, may hold values from -1 to 1
Outputs:
- attended: bfloat16 [64, 128, 8192], P('resp', None, 'ctx')
- relative: float32 [64], replicated
Inputs may be any that keep to these rules, and one draw needn't show every extreme that they name: `span_ids`: each response names 2 different spans. Among the 8 responses of one group (aligned blocks of rows) no span is named by more than 2 responses, a bound that some block reaches.
All inputs are finite; a program needn't handle non-finite values.
Results may differ from a plain program's by a relative error of at most 0.0059.
Values may be sent and summed in bfloat16 or wider, within the bound.
A program may use at most 64 MiB of HBM per device.

v0:
```python
import math

import jax
import jax.numpy as jnp
from jax import lax
from jax.sharding import PartitionSpec as P

QUERY_HEADS = 64
KEY_HEADS = 8
HEAD_WIDTH = 128
SPAN_LENGTH = 2048
BLK = 64
PICKED_SPANS = 2


def for_sending(value):
    return jax.tree.map(lambda a: a.astype(jnp.bfloat16) if a.dtype == jnp.float32 else a, value)


def local(queries, keys, values, span_ids, lengths, judge):
    ctx_count = lax.axis_size("ctx")
    resp_count, response_token_count, slice_width = queries.shape
    document_row_block = keys.shape[0]
    span_fragments = SPAN_LENGTH // document_row_block
    span_count = ctx_count // span_fragments
    slot_count = min(resp_count, 2 * ((resp_count * PICKED_SPANS + span_count - 1) // span_count))
    queries_per_group = QUERY_HEADS // KEY_HEADS
    head_feats = min(slice_width, HEAD_WIDTH)
    own_heads = slice_width // head_feats
    inverse = 1.0 / math.sqrt(HEAD_WIDTH)
    highest = lax.Precision.HIGHEST
    device = lax.axis_index("ctx")
    first_head = device * slice_width // HEAD_WIDTH
    chosen = jnp.any(
        span_ids[:, :, None] == jnp.arange(span_count, dtype=jnp.int32)[None, None, :], axis=1
    ).astype(jnp.int32)
    order_in = jnp.cumsum(chosen, axis=0) - 1
    owner_table = chosen.T[:, None, :] * (
        order_in.T[:, None, :] == jnp.arange(slot_count, dtype=jnp.int32)[None, :, None]
    ).astype(jnp.int32)
    spread = jnp.repeat(owner_table, span_fragments, axis=0)
    slot_resp = jnp.sum(spread * jnp.arange(resp_count, dtype=jnp.int32)[None, None, :], axis=-1)
    slot_live = jnp.sum(spread, axis=-1) > 0
    key_shard_parts = keys.reshape(document_row_block, KEY_HEADS, HEAD_WIDTH)
    value_shard_parts = values.reshape(document_row_block, KEY_HEADS, HEAD_WIDTH)

    def one_slot(query_rows):
        query_shard_parts = query_rows.reshape(
            response_token_count, KEY_HEADS, queries_per_group, HEAD_WIDTH
        )
        outputs = []
        maxima = []
        totals = []
        for key_head_index in range(KEY_HEADS):
            scores = (
                jnp.einsum(
                    "tjd,pd->jtp",
                    query_shard_parts[:, key_head_index],
                    key_shard_parts[:, key_head_index],
                    preferred_element_type=jnp.float32,
                )
                * inverse
            )
            shard_max = scores.max(-1).astype(jnp.bfloat16)
            max_float = lax.optimization_barrier(shard_max).astype(jnp.float32)
            expo = jnp.exp(scores - max_float[..., None])
            totals.append(jnp.sum(expo, axis=-1).astype(jnp.bfloat16))
            maxima.append(shard_max)
            outputs.append(
                jnp.einsum(
                    "jtp,pd->tjd",
                    expo.astype(jnp.bfloat16),
                    value_shard_parts[:, key_head_index],
                    preferred_element_type=jnp.float32,
                ).astype(jnp.bfloat16)
            )
        shard_out = jnp.stack(outputs, axis=1).reshape(
            response_token_count, QUERY_HEADS * HEAD_WIDTH
        )
        shard_max_all = jnp.stack(maxima, axis=0).reshape(QUERY_HEADS, response_token_count)
        shard_total_all = jnp.stack(totals, axis=0).reshape(QUERY_HEADS, response_token_count)
        return (shard_out, shard_max_all, shard_total_all)

    picked = jnp.take(queries, slot_resp.reshape(-1), axis=0).reshape(
        ctx_count, slot_count, response_token_count, slice_width
    )
    outgoing = jnp.where(slot_live[:, :, None, None], picked, jnp.zeros_like(picked))
    received = lax.all_to_all(outgoing, "ctx", split_axis=0, concat_axis=3, tiled=True)
    item_count = received.shape[1]
    shard_out, shard_max, shard_total = lax.map(
        one_slot, received.reshape(item_count, response_token_count, received.shape[3])
    )
    out_split = shard_out.reshape(slot_count, response_token_count, ctx_count, slice_width)
    part_out = lax.all_to_all(
        for_sending(out_split), "ctx", split_axis=2, concat_axis=2, tiled=True
    ).astype(out_split.dtype)
    every_max, every_total = (
        lax.all_gather(for_sending(shard_max), "ctx", axis=0, tiled=True).astype(shard_max.dtype),
        lax.all_gather(for_sending(shard_total), "ctx", axis=0, tiled=True).astype(
            shard_total.dtype
        ),
    )
    mine = first_head + jnp.arange(own_heads, dtype=jnp.int32)
    part_max = jnp.transpose(
        jnp.take(
            every_max.reshape(ctx_count, slot_count, QUERY_HEADS, response_token_count),
            mine,
            axis=2,
        ),
        (1, 2, 0, 3),
    )
    part_total = jnp.transpose(
        jnp.take(
            every_total.reshape(ctx_count, slot_count, QUERY_HEADS, response_token_count),
            mine,
            axis=2,
        ),
        (1, 2, 0, 3),
    )
    valid = jnp.transpose(spread, (2, 1, 0))
    max_float = part_max.astype(jnp.float32)
    masked = jnp.where(valid[:, :, None, :, None] > 0, max_float[None], -jnp.inf)
    top = masked.max(axis=(1, 3))
    rescale = jnp.exp(masked - top[:, None, :, None, :])
    denom = jnp.einsum(
        "isknt,sknt->ikt", rescale, part_total.astype(jnp.float32), precision=highest
    )
    out_view = part_out.reshape(slot_count, response_token_count, ctx_count, own_heads, head_feats)

    def add_slot(running, pair):
        weight_slot, out_slot = pair
        return (
            running
            + jnp.einsum(
                "iknt,tnkf->itkf", weight_slot, out_slot.astype(jnp.float32), precision=highest
            ),
            None,
        )

    start_sum = jnp.zeros((resp_count, response_token_count, own_heads, head_feats), jnp.float32)
    numer, unused = lax.scan(add_slot, start_sum, (jnp.moveaxis(rescale, 1, 0), out_view))
    combined = (numer / jnp.transpose(denom, (0, 2, 1))[..., None]).reshape(
        resp_count, response_token_count, slice_width
    )
    live = jnp.arange(response_token_count, dtype=jnp.int32)[None, :] < BLK * lengths[:, None]
    attended = jnp.where(live[:, :, None], combined, 0.0).astype(jnp.bfloat16)
    judge_part = lax.dynamic_slice_in_dim(judge, device * slice_width, slice_width)
    dots = jnp.einsum("rtw,w->rt", attended.astype(jnp.float32), judge_part, precision=highest)
    partial_sum = jnp.sum(jnp.where(live, dots, 0.0), axis=1)
    summed = lax.psum(partial_sum, "ctx")
    score = summed / (BLK * lengths).astype(jnp.float32)
    every_score = lax.all_gather(score, "resp", axis=0, tiled=True)
    relative = every_score - jnp.mean(every_score)
    return (attended, relative)


def solution(mesh):
    return jax.shard_map(
        local,
        mesh=mesh,
        in_specs=(
            P("resp", None, "ctx"),
            P("ctx", None),
            P("ctx", None),
            P("resp", None),
            P("resp"),
            P(),
        ),
        out_specs=(P("resp", None, "ctx"), P()),
        check_vma=False,
    )
```

profile of v0, /device:TPU:1, one launch (start us, length us, event | category | flops | bytes accessed | tf_op | source)
XLA Modules:
  0.0 668.8 jit_solution(4121405424332548547)
XLA Ops:
  8.8 3.0 gather_fusion
  11.8 6.4 copy.131
  18.5 3.9 select_select_fusion
  22.3 17.5 %all-to-all-start = ((bf16[64,2,128,128]{2,3,1,0:T(8,128)(2,1)}), bf16[64,2,128,128]{2,3,1,0:T(8,128)(2,1)}, u32[]{:S(2)}, u32[]{:S(2)}) async-start(bf16[64,2,128,128]{2,3,1,0:T(8,128)(2,1)} %select_select_fusion), calls=%async_computation | async-start | bytes 8388608 | tf_op jit(solution)/shard_map/all_to_all | solution.py:88
  42.4 104.5 %all-to-all-done = bf16[64,2,128,128]{2,3,1,0:T(8,128)(2,1)} async-done(((bf16[64,2,128,128]{2,3,1,0:T(8,128)(2,1)}), bf16[64,2,128,128]{2,3,1,0:T(8,128)(2,1)}, u32[]{:S(2)}, u32[]{:S(2)}) %all-to-all-start) | async-done | bytes 4194336 | tf_op jit(solution)/shard_map/all_to_all | solution.py:88
  146.9 4.7 copy.132
  151.6 52.2 %while.26 = (s32[]{:T(128)}, bf16[2,128,8192]{1,2,0:T(8,128)(2,1)}, bf16[2,64,128]{2,1,0:T(8,128)(2,1)S(1)}, bf16[2,64,128]{2,1,0:T(8,128)(2,1)S(1)}, bf16[2,128...) while((s32[]{:T(128)}, bf16[2,128,8192]{1,2,0:T(8,128)(2,1)}, ...), condition=%wide.region_21.22_spmd, body=%wide.region_4.21_spmd.sunk | while | flops 2182078464 | bytes 73679480 | solution.py:90
  151.6 1.7 constant_dynamic-slice_fusion.4
  153.4 1.6 bitcast_reduce_fusion.16
  159.8 1.5 bitcast_reduce_fusion.19
  166.3 1.5 bitcast_reduce_fusion.22
  177.7 1.7 constant_dynamic-slice_fusion.4
  179.5 1.6 bitcast_reduce_fusion.16
  204.4 6.4 copy.136
  210.9 28.8 %all-to-all-start.1 = ((bf16[2,128,64,128]{3,1,0,2:T(8,128)(2,1)}), bf16[2,128,64,128]{3,1,0,2:T(8,128)(2,1)}, u32[]{:S(2)}, u32[]{:S(2)}) async-start(bf16[2,128,64,128]{3,1,0,2:T(8,128)(2,1)} %copy.136), calls=%async_computation.1 | async-start | bytes 8388608 | tf_op jit(solution)/shard_map/all_to_all | solution.py:94
  242.1 160.1 %all-gather.3.cloned.1.call-done = bf16[128,64,128]{2,1,0:T(8,128)(2,1)} async-done(((bf16[2,64,128]{2,1,0:T(8,128)(2,1)}), bf16[128,64,128]{2,1,0:T(8,128)(2,1)}) %all-gather.3.cloned.1.call-update) | async-done | bytes 2097168 | tf_op jit(solution)/shard_map/all_gather | solution.py:98
  402.2 83.6 %all-gather.5.cloned.1.call-done = bf16[128,64,128]{2,1,0:T(8,128)(2,1)} async-done(((bf16[2,64,128]{2,1,0:T(8,128)(2,1)}), bf16[128,64,128]{2,1,0:T(8,128)(2,1)}) %all-gather.5.cloned.1.call-update) | async-done | bytes 2097168 | tf_op jit(solution)/shard_map/all_gather | solution.py:99
  488.9 11.8 %while.27 = (s32[]{:T(128)}, f32[8,128,1,128]{3,0,1,2:T(8,128)S(1)}, bf16[2,128,64,1,128]{4,1,0,2,3:T(8,128)(2,1)}, f32[2,8,1,64,128]{3,1,4,2,0:T(8,128)}, s32[]{:T(128)}, /*index=5*/s32[]{:T(128)}) while((s32[]{:T(128)}, f32[8,128,1,128]{3,0,1,2:T(8,128)S(1)}, bf16[2,128,64,1,128]{4,1,0,2,3:T(8,128)(2,1)}, ...), condition=%wide.region_24.26_spmd.clone, body=%wide.region_23.25_spmd.clone.sunk | while | flops 100925440 | bytes 7864915 | solution.py:141
  488.9 1.7 constant_dynamic-slice_fusion.5
  490.7 4.1 fusion.200
  494.8 1.7 constant_dynamic-slice_fusion.5
  496.6 4.1 fusion.200
  503.0 113.3 %psum.7 = f32[8]{0:T(128)S(1)} all-reduce(f32[8]{0:T(128)S(1)} %select_reduce_fusion.1), channel_id=1, replica_groups=mesh['ctx'=64,'resp'=8] {'ctx'}, use_global_device_ids=true, to_apply=%region_26.28 | all-reduce | flops 8 | bytes 64 | tf_op jit(solution)/shard_map/psum | solution.py:150
  616.4 43.8 %all-reduce = f32[64]{0:T(128)S(1)} all-reduce(f32[64]{0:T(128)S(1)} %divide_dynamic-update-slice_fusion), channel_id=1, replica_groups=mesh['ctx'=64,'resp'=8] {'resp'}, use_global_device_ids=true, to_apply=%add | all-reduce | flops 64 | bytes 512
  (170 shorter events, 55.5 us)
Async XLA Ops:
  7.2 1.6 copy-start
  22.3 17.6 %copy-start.3 = (bf16[512,1024]{1,0:T(8,128)(2,1)S(1)}, bf16[512,1024]{1,0:T(8,128)(2,1)}, u32[]{:S(2)}) copy-start(bf16[512,1024]{1,0:T(8,128)(2,1)} %param.13) | copy-start | bytes 3145732
  22.3 124.6 %all-to-all-start = ((bf16[64,2,128,128]{2,3,1,0:T(8,128)(2,1)}), bf16[64,2,128,128]{2,3,1,0:T(8,128)(2,1)}, u32[]{:S(2)}, u32[]{:S(2)}) async-start(bf16[64,2,128,128]{2,3,1,0:T(8,128)(2,1)} %select_select_fusion), calls=%async_computation | async-start | bytes 8388608 | tf_op jit(solution)/shard_map/all_to_all | solution.py:88
  39.9 362.3 %all-gather.3.cloned.1.call-start = ((), (), s32[]{:S(2)}) async-start(), calls=%async_computation.2 | async-start | bytes 2129920 | tf_op jit(solution)/shard_map/all_gather | solution.py:98
  40.0 1.9 copy-start.4
  153.4 2.2 copy-start.2
  179.4 2.2 copy-start.2
  203.8 0.6 copy-start.6
  203.8 7.0 %copy-start.7 = (bf16[2,64,128]{2,1,0:T(8,128)(2,1)}, bf16[2,64,128]{2,1,0:T(8,128)(2,1)S(1)}, u32[]{:S(2)}) copy-start(bf16[2,64,128]{2,1,0:T(8,128)(2,1)S(1)} %get-tuple-element.67) | copy-start | bytes 98308
  210.9 31.1 %copy-start.8 = (s32[8]{0:T(128)S(1)}, s32[8]{0:T(128)}, u32[]{:S(2)}) copy-start(s32[8]{0:T(128)} %param.16) | copy-start | bytes 100
  210.9 278.1 %all-to-all-start.1 = ((bf16[2,128,64,128]{3,1,0,2:T(8,128)(2,1)}), bf16[2,128,64,128]{3,1,0,2:T(8,128)(2,1)}, u32[]{:S(2)}, u32[]{:S(2)}) async-start(bf16[2,128,64,128]{3,1,0,2:T(8,128)(2,1)} %copy.136), calls=%async_computation.1 | async-start | bytes 8388608 | tf_op jit(solution)/shard_map/all_to_all | solution.py:94
  239.7 246.1 %all-gather.5.cloned.1.call-start = ((), (), s32[]{:S(2)}) async-start(), calls=%async_computation.3 | async-start | bytes 2129920 | tf_op jit(solution)/shard_map/all_gather | solution.py:99
  500.7 161.3 %copy-start.1 = (bf16[8,128,128]{2,1,0:T(8,128)(2,1)S(1)}, bf16[8,128,128]{2,1,0:T(8,128)(2,1)}, u32[]{:S(2)}) copy-start(bf16[8,128,128]{2,1,0:T(8,128)(2,1)} %param.12) | copy-start | bytes 786436
  501.1 160.9 %copy-start.5 = (bf16[8,128,128]{2,1,0:T(8,128)(2,1)}, bf16[8,128,128]{2,1,0:T(8,128)(2,1)S(1)}, u32[]{:S(2)}) copy-start(bf16[8,128,128]{2,1,0:T(8,128)(2,1)S(1)} %fusion.120) | copy-start | bytes 786436
Sparse Core Ops, SparseCore 0:
  204.6 197.5 all-gather.2
  405.2 80.4 all-gather.4
where the time goes:
time: 670 us; the launch traced here: 669 us
  waiting for transfers between devices  349 us (52%)
  blocking collectives  157 us (23%)
  starting transfers between devices  46.4 us (7%)
  matrix products  44.8 us (7%)
  local copies, waits for them, and re-layouts  36.4 us (5%)
  other arithmetic  19.3 us (3%)
  between operations  15.6 us (2%)
    all_gather x1, waiting for transfers between devices, local(): lax.all_gather(for_sending(shard_max), 'ctx', axis=0, tiled=True)  160 us
    psum x1, blocking collectives, local(): summed = lax.psum(partial_sum, 'ctx')  113 us
    all_to_all x1, waiting for transfers between devices, local(): lax.all_to_all(outgoing, 'ctx', split_axis=0, concat_axis=3, tiled=True)  104 us
    all_gather x1, waiting for transfers between devices, local(): lax.all_gather(for_sending(shard_total), 'ctx', axis=0, tiled=True)  83.6 us
    unnamed x1, blocking collectives  43.8 us
    all_to_all x1, starting transfers between devices, local(): lax.all_to_all(for_sending(out_split), 'ctx', split_axis=2, concat_axis=2...  28.8 us
    dot_general x16, matrix products, one_slot(): jnp.einsum('tjd,pd->jtp', query_shard_parts[:, key_head_index], key_shard...  24.4 us
    all_to_all x1, starting transfers between devices, local(): lax.all_to_all(outgoing, 'ctx', split_axis=0, concat_axis=3, tiled=True)  17.5 us
  transfers between devices with their start and end apart: 4, of which 3 were waited for; matrix products, arithmetic and copies ran while one was open for 2% of the time, Pallas kernels for 0%

commit v1 on v0

v1 whole, which is shorter than its diff:
```python
import math

import jax
import jax.numpy as jnp
from jax import lax
from jax.experimental import pallas as pl
from jax.experimental.pallas import tpu as pltpu
from jax.sharding import PartitionSpec as P

MESH = pl.DeviceIdType.MESH
NZ, NY, NX, NC = 8, 8, 4, 2
NG = NX * NC
HEAD = 128
TOK = 128
RESP = 8
BLK = 64
POS = 64
SCALE = math.log2(math.e) / math.sqrt(HEAD)
BF = jnp.bfloat16
F32 = jnp.float32


def kernel(
    q_ref, k_ref, v_ref, span_ref, len_ref, judge_ref,
    att_ref, rel_ref,
    kbuf, vbuf, vstage, vtb, qbuf, idbuf, idsm, pbuf, sstat, rstat, obuf, rbuf, t1, t2, t3,
    local_sem, zsend, zrecv, ysend, yrecv, csend, crecv, qsend, qrecv, idsend, idrecv,
    ssend, srecv, osend, orecv, rsend, rrecv,
):
    n = lax.axis_index("ctx")
    g = lax.axis_index("resp")
    z, y = n // NY, n % NY
    x, c = g // NC, g % NC
    half, quarter = y // 4, y % 4

    def at_z(zz):
        return (zz * NY + y, g)

    def at_y(yy):
        return (z * NY + yy, g)

    def at_g(gg):
        return (n, gg)

    def remote(src, dst, ss, rs, dev):
        return pltpu.make_async_remote_copy(
            src_ref=src, dst_ref=dst, send_sem=ss, recv_sem=rs, device_id=dev, device_id_type=MESH
        )

    sent = []

    def send(src, dst, ss, rs, dev):
        copy = remote(src, dst, ss, rs, dev)
        copy.start()
        sent.append(copy)

    def arrived(dst, rs):
        remote(dst, dst, rs, rs, at_g(g)).wait_recv()

    rows = pl.ds(pl.multiple_of(x * 128, 128), 128)
    krows = pl.ds(pl.multiple_of(x * 128 + c * POS, POS), POS)

    def cols(zz):
        return pl.ds(pl.multiple_of(zz * HEAD, HEAD), HEAD)

    vload = pltpu.make_async_copy(v_ref.at[rows, :], vstage, local_sem.at[0])
    vload.start()
    kown = pltpu.make_async_copy(
        k_ref.at[krows, cols(z)], kbuf.at[z, half, quarter, c], local_sem.at[1]
    )
    kown.start()
    qown = pltpu.make_async_copy(q_ref, qbuf.at[0], local_sem.at[2])
    qown.start()
    idbuf[0] = span_ref[...]

    barrier = pltpu.get_barrier_semaphore()
    for d in range(1, NZ):
        pl.semaphore_signal(barrier, inc=1, device_id=at_z((z + d) % NZ), device_id_type=MESH)
    for d in range(1, NY):
        pl.semaphore_signal(barrier, inc=1, device_id=at_y((y + d) % NY), device_id_type=MESH)
    for d in range(1, NG):
        pl.semaphore_signal(barrier, inc=1, device_id=at_g((g + d) % NG), device_id_type=MESH)
    pl.semaphore_wait(barrier, NZ + NY + NG - 3)

    for d in range(1, NZ):
        zz = (z + d) % NZ
        send(
            k_ref.at[krows, cols(zz)], kbuf.at[z, half, quarter, c],
            zsend.at[0, d], zrecv.at[0, d], at_z(zz),
        )
    for d in (2, 1, 3):
        dev = at_g(((x + d) % NX) * NC + c)
        send(idbuf.at[0], idbuf.at[4 - d], idsend.at[d], idrecv.at[4 - d], dev)
        send(q_ref, qbuf.at[4 - d], qsend.at[d], qrecv.at[4 - d], dev)
    vload.wait()
    for j in range(NZ):
        vtb[j] = jnp.transpose(vstage[:, j * HEAD:(j + 1) * HEAD]).reshape(2, POS, 128)
    vbuf[z, half, quarter, c] = vtb[z, c]
    for d in range(1, NZ):
        zz = (z + d) % NZ
        send(
            vtb.at[zz, c], vbuf.at[z, half, quarter, c],
            zsend.at[1, d], zrecv.at[1, d], at_z(zz),
        )

    bufs = (kbuf, vbuf)

    def piece(w, yy, p):
        return bufs[w].at[pl.ds(4 * p, 4), yy // 4, yy % 4, c]

    def valid(way, t, p):
        return t < 3 or p == way

    def to_next(w, way, t, p):
        yy = (y + (NY - t if way == 0 else t)) % NY
        dev = at_y((y + (1 if way == 0 else NY - 1)) % NY)
        ref = piece(w, yy, p)
        send(ref, ref, ysend.at[w, way, t, p], yrecv.at[w, way, t, p], dev)

    sibling = at_g(x * NC + (1 - c))

    def to_sibling(w, number, yy, p):
        ref = piece(w, yy, p)
        send(ref, ref, csend.at[w, number, p], crecv.at[w, number, p], sibling)

    def own_chunk(w):
        for d in range(1, NZ):
            arrived(bufs[w].at[(z + NZ - d) % NZ, half, quarter, c], zrecv.at[w, d])
        for p in range(2):
            for way in range(2):
                to_next(w, way, 0, p)
        for p in range(2):
            to_sibling(w, 0, y, p)

    def ring_step(w, t):
        for p in range(2):
            for way in range(2):
                if not valid(way, t, p):
                    continue
                yy = (y + (NY - 1 - t if way == 0 else 1 + t)) % NY
                arrived(piece(w, yy, p), yrecv.at[w, way, t, p])
                if t < 3 and valid(way, t + 1, p):
                    to_next(w, way, t + 1, p)
                to_sibling(w, (1 + 3 * way + t) if t < 3 else 7, yy, p)

    def from_sibling(w):
        for number in range(8):
            if number == 0:
                yy = y
            elif number < 4:
                yy = (y + NY - number) % NY
            elif number < 7:
                yy = (y + number - 3) % NY
            else:
                yy = (y + 4) % NY
            for p in range(2):
                arrived(
                    bufs[w].at[pl.ds(4 * p, 4), yy // 4, yy % 4, 1 - c], crecv.at[w, number, p]
                )

    kown.wait()
    own_chunk(0)
    own_chunk(1)
    for t in range(4):
        ring_step(0, t)
    qown.wait()
    for e in range(1, NX):
        arrived(idbuf.at[e], idrecv.at[e])
        arrived(qbuf.at[e], qrecv.at[e])
    ids = pltpu.make_async_copy(idbuf, idsm, local_sem.at[3])
    ids.start()
    ids.wait()
    from_sibling(0)

    def scores(e):
        def one(r, carry):
            q = qbuf[e, r]
            raw = []
            for k in range(2):
                s = idsm[e, r, k]
                keys = kbuf[s // 2, s % 2].reshape(512, HEAD)
                raw.append(
                    lax.dot_general(keys, q, (((1,), (1,)), ((), ())), preferred_element_type=F32)
                )
            top = jnp.maximum(
                jnp.max(raw[0], axis=0, keepdims=True), jnp.max(raw[1], axis=0, keepdims=True)
            )
            total = jnp.zeros((1, TOK), F32)
            for k in range(2):
                expo = jnp.exp2((raw[k] - top) * SCALE)
                total = total + jnp.sum(expo, axis=0, keepdims=True)
                pbuf[e, r, k] = expo.astype(BF)
            sstat[e, 0, pl.ds(r, 1), :] = top
            sstat[e, 1, pl.ds(r, 1), :] = total
            return carry

        lax.fori_loop(0, RESP, one, 0)

    for t, e in enumerate((2, 1, 3, 0)):
        ring_step(1, t)
        scores(e)
        if e:
            send(
                sstat.at[e], rstat.at[4 - e], ssend.at[e], srecv.at[4 - e],
                at_g(((x + e) % NX) * NC + c),
            )
    rstat[0] = sstat[0]
    from_sibling(1)

    def out_copy(e, r):
        return remote(
            obuf.at[e, r], rbuf.at[(4 - e) % 4, r], osend.at[e, r], orecv.at[(4 - e) % 4, r],
            at_g(((x + e) % NX) * NC + c),
        )

    def outputs(e):
        def one(r, carry):
            parts = []
            for k in range(2):
                s = idsm[e, r, k]
                vals = vbuf[s // 2, s % 2].reshape(4, HEAD, 128)
                parts += [vals[i] for i in range(4)]
            vt = jnp.concatenate(parts, axis=1)
            out = jnp.dot(vt, pbuf[e, r].reshape(1024, TOK), preferred_element_type=F32)
            out = (out * (1.0 / sstat[e, 1, pl.ds(r, 1), :])).astype(BF)
            if e:
                obuf[e, r] = out
                out_copy(e, r).start()
            else:
                rbuf[0, r] = out
            return carry

        lax.fori_loop(0, RESP, one, 0)

    for e in (2, 1, 3, 0):
        outputs(e)

    for e in range(1, NX):
        arrived(rstat.at[e], srecv.at[e])
    tops = rstat[:, 0]
    weight = jnp.exp2((tops - jnp.max(tops, axis=0, keepdims=True)) * SCALE) * rstat[:, 1]
    weight = weight / jnp.sum(weight, axis=0, keepdims=True)
    rstat[:, 0] = weight
    judge = jnp.transpose(jnp.broadcast_to(judge_ref[pl.ds(n, 1), :], (TOK, HEAD)))
    token = lax.broadcasted_iota(jnp.int32, (HEAD, TOK), 1)

    def combine(r, carry):
        total = jnp.zeros((HEAD, TOK), F32)
        for e in range(NX):
            if e:
                arrived(rbuf.at[e, r], orecv.at[e, r])
            total = total + rstat[e, 0, pl.ds(r, 1), :] * rbuf[e, r].astype(F32)
        total = jnp.where(token < BLK * len_ref[r], total, 0.0).astype(BF)
        att_ref[r] = jnp.transpose(total)
        t1[z, pl.ds(r, 1), :] = jnp.sum(total.astype(F32) * judge, axis=0, keepdims=True)
        return carry

    lax.fori_loop(0, RESP, combine, 0)

    def spread(number, buf, own, size, where):
        for d in range(1, size):
            send(
                buf.at[own], buf.at[own], rsend.at[number, d], rrecv.at[number, d],
                where((own + d) % size),
            )
        for d in range(1, size):
            arrived(buf.at[(own + size - d) % size], rrecv.at[number, d])

    spread(0, t1, z, NZ, at_z)
    t2[y] = jnp.sum(t1[...], axis=0)
    spread(1, t2, y, NY, at_y)
    dots = jnp.sum(jnp.sum(t2[...], axis=0), axis=1, keepdims=True)
    row = lax.broadcasted_iota(jnp.int32, (RESP, 128), 0)
    lane = lax.broadcasted_iota(jnp.int32, (RESP, 128), 1)
    tokens = jnp.ones((RESP, 128), F32)
    for r in range(RESP):
        tokens = jnp.where(row == r, (BLK * len_ref[r]).astype(F32), tokens)
    t3[g] = jnp.broadcast_to(dots, (RESP, 128)) / tokens
    spread(2, t3, g, NG, at_g)
    flat = jnp.zeros((RESP, 128), F32)
    for i in range(NG):
        flat = flat + jnp.where(lane == i * RESP + row, t3[i], 0.0)
    flat = jnp.sum(flat, axis=0, keepdims=True)
    rel_ref[...] = flat - jnp.sum(flat, axis=1, keepdims=True) / (NG * RESP)

    for copy in sent:
        copy.wait_send()

    def drain(r, carry):
        for e in range(1, NX):
            out_copy(e, r).wait_send()
        return carry

    lax.fori_loop(0, RESP, drain, 0)


def local(queries, keys, values, span_ids, lengths, judge):
    vmem = pl.BlockSpec(memory_space=pltpu.VMEM)
    smem = pl.BlockSpec(memory_space=pltpu.SMEM)
    hbm = pl.BlockSpec(memory_space=pl.ANY)
    dma = pltpu.SemaphoreType.DMA
    attended, relative = pl.pallas_call(
        kernel,
        out_shape=(
            jax.ShapeDtypeStruct((RESP, TOK, HEAD), BF),
            jax.ShapeDtypeStruct((1, 128), F32),
        ),
        in_specs=[hbm, hbm, hbm, vmem, smem, vmem],
        out_specs=(vmem, vmem),
        scratch_shapes=[
            pltpu.VMEM((NZ, 2, 4, 2, POS, HEAD), BF),
            pltpu.VMEM((NZ, 2, 4, 2, POS, 128), BF),
            pltpu.VMEM((128, NZ * HEAD), BF),
            pltpu.VMEM((NZ, 2, POS, 128), BF),
            pltpu.VMEM((NX, RESP, TOK, HEAD), BF),
            pltpu.VMEM((NX, RESP, 2), jnp.int32),
            pltpu.SMEM((NX, RESP, 2), jnp.int32),
            pltpu.VMEM((NX, RESP, 2, 512, TOK), BF),
            pltpu.VMEM((NX, 2, RESP, TOK), F32),
            pltpu.VMEM((NX, 2, RESP, TOK), F32),
            pltpu.VMEM((NX, RESP, HEAD, TOK), BF),
            pltpu.VMEM((NX, RESP, HEAD, TOK), BF),
            pltpu.VMEM((NZ, RESP, TOK), F32),
            pltpu.VMEM((NY, RESP, TOK), F32),
            pltpu.VMEM((NG, RESP, TOK), F32),
            dma((4,)),
            dma((2, NZ)),
            dma((2, NZ)),
            dma((2, 2, 4, 2)),
            dma((2, 2, 4, 2)),
            dma((2, 8, 2)),
            dma((2, 8, 2)),
            dma((NX,)),
            dma((NX,)),
            dma((NX,)),
            dma((NX,)),
            dma((NX,)),
            dma((NX,)),
            dma((NX, RESP)),
            dma((NX, RESP)),
            dma((3, 8)),
            dma((3, 8)),
        ],
        compiler_params=pltpu.CompilerParams(
            collective_id=0, has_side_effects=True, vmem_limit_bytes=40 * 1024 * 1024
        ),
    )(queries, keys, values, span_ids, lengths, judge.reshape(NZ * NY, HEAD))
    return attended, relative[0, :NG * RESP]


def solution(mesh):
    return jax.shard_map(
        local,
        mesh=mesh,
        in_specs=(
            P("resp", None, "ctx"),
            P("ctx", None),
            P("ctx", None),
            P("resp", None),
            P("resp"),
            P(),
        ),
        out_specs=(P("resp", None, "ctx"), P()),
        check_vma=False,
    )
```

time: 670 us -> 93.8 us (0.14)
  waiting for transfers between devices: 349 us -> 0 us
  blocking collectives: 157 us -> 0 us
  Pallas kernels: 0 us -> 86.1 us
  starting transfers between devices: 46.4 us -> 0 us
  matrix products: 44.8 us -> 0 us
  local copies, waits for them, and re-layouts: 36.4 us -> 6.7 us
  other arithmetic: 19.3 us -> 0 us
  between operations: 15.6 us -> 0.65 us
    all_gather x2 -> x0, waiting for transfers between devices: 244 us -> none  [the longest x1 160 us: local(): lax.all_gather(for_sending(shard_max), 'ctx', axis=0, tiled=True)]
    psum x1 -> x0, blocking collectives: 113 us -> none  [local(): summed = lax.psum(partial_sum, 'ctx')]
    all_to_all x2 -> x0, waiting for transfers between devices: 104 us -> none  [the longest x1 104 us: local(): lax.all_to_all(outgoing, 'ctx', split_axis=0, concat_axis=3, tiled=True)]
    pallas_call x0 -> x1, Pallas kernels: none -> 86.1 us  [local(): pl.pallas_call(kernel, out_shape=(jax.ShapeDtypeStruct((RESP, TOK, HEAD),...]
    all_to_all x2 -> x0, starting transfers between devices: 46.3 us -> none  [the longest x1 28.8 us: local(): lax.all_to_all(for_sending(out_split), 'ctx', split_axis=2, concat_axis=2...]
    dot_general x35 -> x0, matrix products: 44.8 us -> none  [the longest x16 24.4 us: one_slot(): jnp.einsum('tjd,pd->jtp', query_shard_parts[:, key_head_index], key_shard...]
    unnamed x1 -> x0, blocking collectives: 43.8 us -> none
    reduce_sum x20 -> x0, other arithmetic: 10.5 us -> none  [the longest x16 9.56 us: one_slot(): totals.append(jnp.sum(expo, axis=-1).astype(jnp.bfloat16))]
  transfers between devices with their start and end apart: 4 -> 0, of which waited for: 3 -> 0; matrix products, arithmetic and copies ran while one was open for 2% -> 0% of each run, Pallas kernels for 0% -> 0%
where the time goes in v1:
time: 93.8 us; the launch traced here: 93.5 us
  Pallas kernels  86.1 us (92%)
  local copies, waits for them, and re-layouts  6.7 us (7%)
    pallas_call x1, Pallas kernels, local(): pl.pallas_call(kernel, out_shape=(jax.ShapeDtypeStruct((RESP, TOK, HEAD),...  86.1 us
    unnamed x14, local copies, waits for them, and re-layouts  6.18 us

profile of v1, /device:TPU:1, one launch (start us, length us, event | category | flops | bytes accessed | tf_op | source)
XLA Modules:
  0.0 93.5 jit_solution(5719929113901275024)
XLA Ops:
  0.6 0.0 copy-start.5
  0.6 0.7 copy-done.5
  1.3 0.0 copy-start.4
  1.3 0.1 copy.8.span_ref
  1.4 0.6 copy-done.4
  2.0 0.0 copy-start
  2.0 1.2 %copy-done = bf16[512,1024]{1,0:T(8,128)(2,1)S(1)} copy-done((bf16[512,1024]{1,0:T(8,128)(2,1)S(1)}, bf16[512,1024]{1,0:T(8,128)(2,1)}, u32[]{:S(2)}) %copy-start) | copy-done | bytes 1048600
  3.2 0.0 copy-start.1
  3.2 1.2 %copy-done.1 = bf16[512,1024]{1,0:T(8,128)(2,1)S(1)} copy-done((bf16[512,1024]{1,0:T(8,128)(2,1)S(1)}, bf16[512,1024]{1,0:T(8,128)(2,1)}, u32[]{:S(2)}) %copy-start.1) | copy-done | bytes 1048600
  4.4 0.0 copy-start.2
  4.4 0.9 %copy-done.2 = bf16[8,128,128]{2,1,0:T(8,128)(2,1)S(1)} copy-done((bf16[8,128,128]{2,1,0:T(8,128)(2,1)S(1)}, bf16[8,128,128]{2,1,0:T(8,128)(2,1)}, u32[]{:S(2)}) %copy-start.2) | copy-done | bytes 262168
  5.4 0.0 copy-start.3
  5.4 0.8 copy-done.3
  6.1 86.1 %shard_map.77 = (bf16[8,128,128]{2,1,0:T(8,128)(2,1)S(1)}, f32[1,128]{1,0:T(1,128)S(1)}) custom-call(bf16[8,128,128]{2,1,0:T(8,128)(2,1)S(1)} %copy-done.2, bf16[512,1024]{1,0:T(8,128)(2,1)S(1)} %copy-done, bf16[512,1024]{1,0:T(8,128)(2,1)S(1)} %copy-done.1, s32[8,2]{1,0:T(8,128)S(1)} %copy.8.span_ref, s32[8]{0:T(128)S(1)} %copy-done.4, f32[64,128]{1,0:T(8,128)S(1)} %bitcast.3), custom_call_target="tpu_custom_call" | custom-call | tf_op jit(solution)/shard_map/pallas_call | solution.py:302
  92.2 0.5 slice_bitcast_fusion
  92.8 0.7 copy.10
Async XLA Ops:
  0.6 0.7 copy-start.5
  1.3 0.7 copy-start.4
  2.0 1.2 %copy-start = (bf16[512,1024]{1,0:T(8,128)(2,1)S(1)}, bf16[512,1024]{1,0:T(8,128)(2,1)}, u32[]{:S(2)}) copy-start(bf16[512,1024]{1,0:T(8,128)(2,1)} %k_ref.1) | copy-start | bytes 3145732
  3.2 1.2 %copy-start.1 = (bf16[512,1024]{1,0:T(8,128)(2,1)S(1)}, bf16[512,1024]{1,0:T(8,128)(2,1)}, u32[]{:S(2)}) copy-start(bf16[512,1024]{1,0:T(8,128)(2,1)} %v_ref.1) | copy-start | bytes 3145732
  4.4 0.9 %copy-start.2 = (bf16[8,128,128]{2,1,0:T(8,128)(2,1)S(1)}, bf16[8,128,128]{2,1,0:T(8,128)(2,1)}, u32[]{:S(2)}) copy-start(bf16[8,128,128]{2,1,0:T(8,128)(2,1)} %q_ref.1) | copy-start | bytes 786436
  5.4 0.8 copy-start.3

commit v2 on v1

v2 whole, which is shorter than its diff:
```python
import math

import jax
import jax.numpy as jnp
from jax import lax
from jax.experimental import pallas as pl
from jax.experimental.pallas import tpu as pltpu
from jax.sharding import PartitionSpec as P

MESH = pl.DeviceIdType.MESH
NZ, NY, NX, NC = 8, 8, 4, 2
NG = NX * NC
HEAD = 128
TOK = 128
RESP = 8
BLK = 64
POS = 64
PIECES = (4, 2)
SCALE = math.log2(math.e) / math.sqrt(HEAD)
BF = jnp.bfloat16
F32 = jnp.float32


def kernel(
    q_ref, k_ref, v_ref, span_ref, len_ref, judge_ref,
    att_ref, rel_ref,
    kb0, kb1, kb2, kb3, vbuf, vstage, vtb, qbuf, idbuf, idsm, pbuf, mq, lq, coef, wmerge,
    sstat, rstat, mstat, obuf, mbuf, rbuf, jbuf, abuf, t1, t2, t3,
    local_sem, zsend, zrecv, ysend, yrecv, csend, crecv, qsend, qrecv, idsend, idrecv,
    ssend, srecv, osend, orecv, asem, rsend, rrecv,
):
    n = lax.axis_index("ctx")
    g = lax.axis_index("resp")
    z, y = n // NY, n % NY
    x, c = g // NC, g % NC
    half, quarter = y // 4, y % 4
    kb = (kb0, kb1, kb2, kb3)

    def at_z(zz):
        return (zz * NY + y, g)

    def at_y(yy):
        return (z * NY + yy, g)

    def at_g(gg):
        return (n, gg)

    def at_x(d):
        return (n, ((x + d) % NX) * NC + c)

    sibling = at_g(x * NC + (1 - c))

    def remote(src, dst, ss, rs, dev):
        return pltpu.make_async_remote_copy(
            src_ref=src, dst_ref=dst, send_sem=ss, recv_sem=rs, device_id=dev, device_id_type=MESH
        )

    sent = []

    def send(src, dst, ss, rs, dev):
        copy = remote(src, dst, ss, rs, dev)
        copy.start()
        sent.append(copy)

    def arrived(dst, rs):
        remote(dst, dst, rs, rs, sibling).wait_recv()

    def drain():
        while sent:
            sent.pop(0).wait_send()

    rows = pl.ds(pl.multiple_of(x * 128, 128), 128)
    krows = pl.ds(pl.multiple_of(x * 128 + c * POS, POS), POS)

    def cols(zz):
        return pl.ds(pl.multiple_of(zz * HEAD, HEAD), HEAD)

    vload = pltpu.make_async_copy(v_ref.at[rows, :], vstage, local_sem.at[0])
    vload.start()
    pltpu.make_async_copy(k_ref.at[krows, cols(z)], kb0.at[z, half, c], zrecv.at[0, 0]).start()
    idload = pltpu.make_async_copy(span_ref, idbuf.at[0], local_sem.at[1])
    idload.start()
    qown = pltpu.make_async_copy(q_ref, qbuf.at[0], local_sem.at[2])
    qown.start()
    jload = pltpu.make_async_copy(
        judge_ref.at[pl.ds(pl.multiple_of(z * NY, NY), NY), :], jbuf, local_sem.at[3]
    )
    jload.start()

    barrier = pltpu.get_barrier_semaphore()
    for d in range(1, NZ):
        pl.semaphore_signal(barrier, inc=1, device_id=at_z((z + d) % NZ), device_id_type=MESH)
    for d in range(1, NY):
        pl.semaphore_signal(barrier, inc=1, device_id=at_y((y + d) % NY), device_id_type=MESH)
    for d in range(1, NG):
        pl.semaphore_signal(barrier, inc=1, device_id=at_g((g + d) % NG), device_id_type=MESH)
    vload.wait()
    for j in range(NZ):
        vtb[j] = jnp.transpose(vstage[:, j * HEAD:(j + 1) * HEAD]).reshape(2, POS, 128)
    pltpu.make_async_copy(vtb.at[z, c], vbuf.at[z, half, quarter, c], zrecv.at[1, 0]).start()
    idload.wait()
    pl.semaphore_wait(barrier, NZ + NY + NG - 3)

    for d in (1, 7, 2, 6, 3, 5, 4):
        zz = (z + d) % NZ
        send(
            k_ref.at[krows, cols(zz)], kb0.at[z, half, c],
            zsend.at[0, d], zrecv.at[0, d], at_z(zz),
        )
    for d in (1, 7, 2, 6, 3, 5, 4):
        zz = (z + d) % NZ
        send(
            vtb.at[zz, c], vbuf.at[z, half, quarter, c],
            zsend.at[1, d], zrecv.at[1, d], at_z(zz),
        )
    for d in (1, 3, 2):
        send(idbuf.at[0], idbuf.at[4 - d], idsend.at[d], idrecv.at[4 - d], at_x(d))
    for d in (1, 3):
        send(q_ref, qbuf.at[4 - d], qsend.at[d], qrecv.at[4 - d], at_x(d))

    def chunk(w, j, zs, yy, cc):
        if w == 0:
            return kb[j % 4].at[zs, yy // 4, cc]
        return vbuf.at[zs, yy // 4, yy % 4, cc]

    def piece(w, j, i, cc):
        count = PIECES[w]
        width = NZ // count
        first = ((z // width + i) % count) * width
        return chunk(w, j, pl.ds(first, width), (y + j + NY) % NY, cc)

    def valid(w, way, t, i):
        return t < 3 or (i < PIECES[w] // 2) == (way == 0)

    def to_next(w, way, t, i):
        j = -t if way == 0 else t
        count = PIECES[w]
        width = NZ // count
        first = ((z // width + i) % count) * width
        dst = chunk(w, j + (-1 if way == 0 else 1), pl.ds(first, width), (y + j + NY) % NY, c)
        dev = at_y((y + (1 if way == 0 else NY - 1)) % NY)
        send(piece(w, j, i, c), dst, ysend.at[w, way, t, i], yrecv.at[w, way, t, i], dev)

    def to_sibling(w, number, j, i):
        ref = piece(w, j, i, c)
        send(ref, ref, csend.at[w, number, i], crecv.at[w, number, i], sibling)

    def own_chunk(w):
        count = PIECES[w]
        width = NZ // count
        for i in range(count):
            for k in range(width):
                zz = ((z // width + i) % count) * width + k
                arrived(chunk(w, 0, zz, y, c), zrecv.at[w, (z + NZ - zz) % NZ])
            for way in range(2):
                to_next(w, way, 0, i)
            to_sibling(w, 0, 0, i)

    def ring_step(w, t):
        for i in range(PIECES[w]):
            for way in range(2):
                if not valid(w, way, t, i):
                    continue
                j = -1 - t if way == 0 else 1 + t
                arrived(piece(w, j, i, c), yrecv.at[w, way, t, i])
                if t < 3 and valid(w, way, t + 1, i):
                    to_next(w, way, t + 1, i)
                to_sibling(w, (1 + 3 * way + t) if t < 3 else 7, j, i)

    def from_sibling(w, number):
        j = (0, -1, -2, -3, 1, 2, 3, 4)[number]
        for i in range(PIECES[w]):
            arrived(piece(w, j, i, 1 - c), crecv.at[w, number, i])

    def forward_queries():
        arrived(qbuf.at[1], qrecv.at[1])
        send(
            qbuf.at[1, pl.ds(4, 4)], qbuf.at[2, pl.ds(4, 4)], qsend.at[2], qrecv.at[2], at_x(3)
        )
        arrived(qbuf.at[3], qrecv.at[3])
        send(
            qbuf.at[3, pl.ds(0, 4)], qbuf.at[2, pl.ds(0, 4)], qsend.at[0], qrecv.at[0], at_x(1)
        )

    def wait_queries():
        qown.wait()
        arrived(qbuf.at[2, pl.ds(4, 4)], qrecv.at[2])
        arrived(qbuf.at[2, pl.ds(0, 4)], qrecv.at[0])
        for e in range(1, NX):
            arrived(idbuf.at[e], idrecv.at[e])
        ids = pltpu.make_async_copy(idbuf, idsm, local_sem.at[1])
        ids.start()
        ids.wait()

    def scores(j):
        def one(item, carry):
            e, r = item // RESP, item % RESP
            keys = []
            for k in range(2):
                s = idsm[e, k, r]
                keys.append(kb[j][s // 2, s % 2].reshape(128, HEAD))
            raw = lax.dot_general(
                jnp.concatenate(keys, axis=0), qbuf[e, r], (((1,), (1,)), ((), ())),
                preferred_element_type=F32,
            )
            top = jnp.max(raw, axis=0, keepdims=True)
            expo = jnp.exp2((raw - top) * SCALE)
            pbuf[e, r, j] = expo.astype(BF)
            mq[j, e, pl.ds(r, 1), :] = top
            lq[j, e, pl.ds(r, 1), :] = jnp.sum(expo, axis=0, keepdims=True)
            return carry

        lax.fori_loop(0, NX * RESP, one, 0, unroll=4)

    own_chunk(0)
    own_chunk(1)
    ring_step(0, 0)
    forward_queries()
    ring_step(1, 0)
    ring_step(0, 1)
    ring_step(1, 1)
    wait_queries()
    from_sibling(0, 2)
    from_sibling(0, 5)
    scores(2)
    ring_step(0, 2)
    ring_step(1, 2)
    for number in (1, 3, 4, 6):
        from_sibling(0, number)
    scores(1)
    scores(3)
    ring_step(0, 3)
    ring_step(1, 3)
    from_sibling(0, 0)
    from_sibling(0, 7)
    scores(0)

    row = lax.broadcasted_iota(jnp.int32, (RESP, 128), 0)
    for e in (2, 1, 3, 0):
        top = jnp.maximum(jnp.maximum(mq[0, e], mq[1, e]), jnp.maximum(mq[2, e], mq[3, e]))
        scale = [jnp.exp2((mq[j, e] - top) * SCALE) for j in range(4)]
        total = sum(scale[j] * lq[j, e] for j in range(4))
        sstat[e, 0] = top
        sstat[e, 1] = total
        if e:
            send(sstat.at[e], rstat.at[4 - e], ssend.at[e], srecv.at[4 - e], at_x(e))
        if e == 2:
            send(sstat.at[2], mstat.at[0], ssend.at[0], srecv.at[0], at_x(1))
            send(sstat.at[2], mstat.at[1], ssend.at[4], srecv.at[4], at_x(3))
        inverse = 1.0 / total
        for j in range(4):
            coef[e, j] = scale[j] * inverse
    rstat[0] = sstat[0]
    for number in range(8):
        from_sibling(1, number)

    def output(e, r):
        out = jnp.zeros((HEAD, TOK), F32)
        for j in range(4):
            vals = []
            for k in range(2):
                s = idsm[e, k, r]
                vals.append(vbuf[s // 2, s % 2, (quarter + j) % 4].reshape(HEAD, 128))
            part = jnp.dot(
                jnp.concatenate(vals, axis=1), pbuf[e, r, j], preferred_element_type=F32
            )
            out = out + part * coef[e, j, pl.ds(r, 1), :]
        return out

    def out_copy(e, r):
        if e == 2:
            return [
                remote(
                    obuf.at[2, rr], mbuf.at[rr], osend.at[2, rr], orecv.at[2, rr], at_x(d)
                )
                for rr, d in ((r, 1), (4 + r, 3))
            ]
        return remote(obuf.at[e, r], rbuf.at[4 - e, r], osend.at[e, r], orecv.at[4 - e, r], at_x(e))

    def opposite(r, carry):
        first, second = output(2, r), output(2, 4 + r)
        obuf[2, r] = first.astype(BF)
        obuf[2, 4 + r] = second.astype(BF)
        for copy in out_copy(2, r):
            copy.start()
        return carry

    def beside(r, carry):
        first, second = output(1, 4 + r), output(3, r)
        obuf[1, 4 + r] = first.astype(BF)
        obuf[3, r] = second.astype(BF)
        out_copy(1, 4 + r).start()
        out_copy(3, r).start()
        return carry

    def merged(r, carry):
        first, second = output(1, r), output(3, 4 + r)
        arrived(mbuf.at[r], orecv.at[2, r])
        arrived(mbuf.at[4 + r], orecv.at[2, 4 + r])
        first = first + mbuf[r].astype(F32) * wmerge[0, pl.ds(r, 1), :]
        second = second + mbuf[4 + r].astype(F32) * wmerge[1, pl.ds(4 + r, 1), :]
        obuf[1, r] = first.astype(BF)
        obuf[3, 4 + r] = second.astype(BF)
        out_copy(1, r).start()
        out_copy(3, 4 + r).start()
        return carry

    def mine(r, carry):
        first, second = output(0, r), output(0, 4 + r)
        rbuf[0, r] = first.astype(BF)
        rbuf[0, 4 + r] = second.astype(BF)
        return carry

    lax.fori_loop(0, 4, opposite, 0)
    lax.fori_loop(0, 4, beside, 0)
    arrived(mstat.at[0], srecv.at[0])
    arrived(mstat.at[1], srecv.at[4])
    for i, e in ((0, 1), (1, 3)):
        top = jnp.maximum(sstat[e, 0], mstat[i, 0])
        here = jnp.exp2((sstat[e, 0] - top) * SCALE) * sstat[e, 1]
        there = jnp.exp2((mstat[i, 0] - top) * SCALE) * mstat[i, 1]
        inverse = 1.0 / (here + there)
        wmerge[i] = there * inverse
        here = jnp.where((row < 4) == (i == 0), here * inverse, 1.0)
        for j in range(4):
            coef[e, j] = coef[e, j] * here
    lax.fori_loop(0, 4, merged, 0)
    lax.fori_loop(0, 4, mine, 0)

    for e in range(1, NX):
        arrived(rstat.at[e], srecv.at[e])
    tops = rstat[:, 0]
    weight = jnp.exp2((tops - jnp.max(tops, axis=0, keepdims=True)) * SCALE) * rstat[:, 1]
    weight = weight / jnp.sum(weight, axis=0, keepdims=True)
    rstat[0, 0] = weight[0]
    rstat[1, 0] = weight[1] + jnp.where(row < 4, 0.0, weight[2])
    rstat[3, 0] = weight[3] + jnp.where(row < 4, weight[2], 0.0)
    jload.wait()
    judge = jnp.transpose(jnp.broadcast_to(jbuf[pl.ds(y, 1), :], (TOK, HEAD)))
    token = lax.broadcasted_iota(jnp.int32, (HEAD, TOK), 1)

    def att_copy(r):
        return pltpu.make_async_copy(abuf.at[r], att_ref.at[r], asem.at[r])

    def combine(r):
        total = rstat[0, 0, pl.ds(r, 1), :] * rbuf[0, r].astype(F32)
        for e in (1, 3):
            arrived(rbuf.at[e, r], orecv.at[e, r])
            total = total + rstat[e, 0, pl.ds(r, 1), :] * rbuf[e, r].astype(F32)
        total = jnp.where(token < BLK * len_ref[r], total, 0.0).astype(BF)
        abuf[r] = jnp.transpose(total)
        att_copy(r).start()
        t1[z, pl.ds(r, 1), :] = jnp.sum(total.astype(F32) * judge, axis=0, keepdims=True)

    def combine_pair(r, carry):
        combine(r)
        combine(4 + r)
        return carry

    lax.fori_loop(0, 4, combine_pair, 0)

    def spread(number, buf, own, size, where):
        copies = []
        for d in range(1, size):
            copy = remote(
                buf.at[own], buf.at[own], rsend.at[number, d], rrecv.at[number, d],
                where((own + d) % size),
            )
            copy.start()
            copies.append(copy)
        drain()
        sent.extend(copies)
        for d in range(1, size):
            arrived(buf.at[(own + size - d) % size], rrecv.at[number, d])

    spread(0, t1, z, NZ, at_z)
    t2[y] = jnp.sum(t1[...], axis=0)
    spread(1, t2, y, NY, at_y)
    dots = jnp.sum(jnp.sum(t2[...], axis=0), axis=1, keepdims=True)
    lane = lax.broadcasted_iota(jnp.int32, (RESP, 128), 1)
    tokens = jnp.ones((RESP, 128), F32)
    for r in range(RESP):
        tokens = jnp.where(row == r, (BLK * len_ref[r]).astype(F32), tokens)
    t3[g] = jnp.broadcast_to(dots, (RESP, 128)) / tokens
    spread(2, t3, g, NG, at_g)
    flat = jnp.zeros((RESP, 128), F32)
    for i in range(NG):
        flat = flat + jnp.where(lane == i * RESP + row, t3[i], 0.0)
    flat = jnp.sum(flat, axis=0, keepdims=True)
    flat = flat - jnp.sum(flat, axis=1, keepdims=True) / (NG * RESP)
    rel_ref[...] = flat[:, :NG * RESP]
    drain()

    def finish(r, carry):
        for copy in out_copy(2, r):
            copy.wait_send()
        for rr in (r, 4 + r):
            out_copy(1, rr).wait_send()
            out_copy(3, rr).wait_send()
            att_copy(rr).wait()
        return carry

    lax.fori_loop(0, 4, finish, 0)


def local(queries, keys, values, span_ids, lengths, judge):
    vmem = pl.BlockSpec(memory_space=pltpu.VMEM)
    smem = pl.BlockSpec(memory_space=pltpu.SMEM)
    hbm = pl.BlockSpec(memory_space=pl.ANY)
    dma = pltpu.SemaphoreType.DMA
    attended, relative = pl.pallas_call(
        kernel,
        out_shape=(
            jax.ShapeDtypeStruct((RESP, TOK, HEAD), BF),
            jax.ShapeDtypeStruct((1, NG * RESP), F32),
        ),
        in_specs=[hbm, hbm, hbm, hbm, smem, hbm],
        out_specs=(hbm, vmem),
        scratch_shapes=[
            pltpu.VMEM((NZ, 2, 2, POS, HEAD), BF),
            pltpu.VMEM((NZ, 2, 2, POS, HEAD), BF),
            pltpu.VMEM((NZ, 2, 2, POS, HEAD), BF),
            pltpu.VMEM((NZ, 2, 2, POS, HEAD), BF),
            pltpu.VMEM((NZ, 2, 4, 2, POS, 128), BF),
            pltpu.VMEM((128, NZ * HEAD), BF),
            pltpu.VMEM((NZ, 2, POS, 128), BF),
            pltpu.VMEM((NX, RESP, TOK, HEAD), BF),
            pltpu.VMEM((NX, 2, RESP), jnp.int32),
            pltpu.SMEM((NX, 2, RESP), jnp.int32),
            pltpu.VMEM((NX, RESP, 4, 256, TOK), BF),
            pltpu.VMEM((4, NX, RESP, TOK), F32),
            pltpu.VMEM((4, NX, RESP, TOK), F32),
            pltpu.VMEM((NX, 4, RESP, TOK), F32),
            pltpu.VMEM((2, RESP, TOK), F32),
            pltpu.VMEM((NX, 2, RESP, TOK), F32),
            pltpu.VMEM((NX, 2, RESP, TOK), F32),
            pltpu.VMEM((2, 2, RESP, TOK), F32),
            pltpu.VMEM((NX, RESP, HEAD, TOK), BF),
            pltpu.VMEM((RESP, HEAD, TOK), BF),
            pltpu.VMEM((NX, RESP, HEAD, TOK), BF),
            pltpu.VMEM((NY, HEAD), F32),
            pltpu.VMEM((RESP, TOK, HEAD), BF),
            pltpu.VMEM((NZ, RESP, TOK), F32),
            pltpu.VMEM((NY, RESP, TOK), F32),
            pltpu.VMEM((NG, RESP, TOK), F32),
            dma((4,)),
            dma((2, NZ)),
            dma((2, NZ)),
            dma((2, 2, 4, 4)),
            dma((2, 2, 4, 4)),
            dma((2, 8, 4)),
            dma((2, 8, 4)),
            dma((NX,)),
            dma((NX,)),
            dma((NX,)),
            dma((NX,)),
            dma((5,)),
            dma((5,)),
            dma((NX, RESP)),
            dma((NX, RESP)),
            dma((RESP,)),
            dma((3, 8)),
            dma((3, 8)),
        ],
        compiler_params=pltpu.CompilerParams(
            collective_id=0, has_side_effects=True, vmem_limit_bytes=60 * 1024 * 1024
        ),
    )(queries, keys, values, span_ids.T, lengths, judge.reshape(NZ * NY, HEAD))
    return attended, relative.reshape(NG * RESP)


def solution(mesh):
    return jax.shard_map(
        local,
        mesh=mesh,
        in_specs=(
            P("resp", None, "ctx"),
            P("ctx", None),
            P("ctx", None),
            P("resp", None),
            P("resp"),
            P(),
        ),
        out_specs=(P("resp", None, "ctx"), P()),
        check_vma=False,
    )
```

time: 93.8 us -> 81.5 us (0.87)
  Pallas kernels: 86.1 us -> 78.5 us
  local copies, waits for them, and re-layouts: 6.7 us -> 2.19 us
    pallas_call x1, Pallas kernels: 86.1 us -> 78.5 us  [local(): pl.pallas_call(kernel, out_shape=(jax.ShapeDtypeStruct((RESP, TOK, HEAD),...]
    unnamed x14 -> x4, local copies, waits for them, and re-layouts: 6.18 us -> 2.19 us
where the time goes in v2:
time: 81.5 us; the launch traced here: 81.3 us
  Pallas kernels  78.5 us (96%)
  local copies, waits for them, and re-layouts  2.19 us (3%)
    pallas_call x1, Pallas kernels, local(): pl.pallas_call(kernel, out_shape=(jax.ShapeDtypeStruct((RESP, TOK, HEAD),...  78.5 us
    unnamed x4, local copies, waits for them, and re-layouts  2.19 us

profile of v2, /device:TPU:1, one launch (start us, length us, event | category | flops | bytes accessed | tf_op | source)
XLA Modules:
  0.0 81.3 jit_solution(5730251469190601860)
XLA Ops:
  0.6 78.5 %shard_map.77 = (bf16[8,128,128]{2,1,0:T(8,128)(2,1)}, f32[1,64]{1,0:T(1,128)}) custom-call(bf16[8,128,128]{2,1,0:T(8,128)(2,1)} %q_ref.1, bf16[512,1024]{1,0:T(8,128)(2,1)} %k_ref.1, bf16[512,1024]{1,0:T(8,128)(2,1)} %v_ref.1, s32[2,8]{1,0:T(2,128)} %bitcast.4, s32[8]{0:T(128)} %len_ref.1, f32[64,128]{1,0:T(8,128)} %bitcast.3), custom_call_target="tpu_custom_call" | custom-call | tf_op jit(solution)/shard_map/pallas_call | solution.py:411
  79.1 0.0 copy-start
  79.1 1.7 %copy.10 = bf16[8,128,128]{2,1,0:T(8,128)(2,1)} copy(bf16[8,128,128]{2,1,0:T(8,128)(2,1)} %get-tuple-element.8) | data formatting | bytes 524288
  80.8 0.0 copy-done
  80.8 0.5 copy.11
Async XLA Ops:
  79.1 1.7 %copy-start = (f32[1,64]{1,0:T(1,128)S(1)}, f32[1,64]{1,0:T(1,128)}, u32[]{:S(2)}) copy-start(f32[1,64]{1,0:T(1,128)} %get-tuple-element.5) | copy-start | bytes 772

commit v3 on v2

--- a/solution.py
+++ b/solution.py
@@ -15,7 +15,7 @@
 RESP = 8
 BLK = 64
 POS = 64
-PIECES = (4, 2)
+PIECES = (4, 4)
 SCALE = math.log2(math.e) / math.sqrt(HEAD)
 BF = jnp.bfloat16
 F32 = jnp.float32
@@ -24,10 +24,10 @@
 def kernel(
     q_ref, k_ref, v_ref, span_ref, len_ref, judge_ref,
     att_ref, rel_ref,
-    kb0, kb1, kb2, kb3, vbuf, vstage, vtb, qbuf, idbuf, idsm, pbuf, mq, lq, coef, wmerge,
-    sstat, rstat, mstat, obuf, mbuf, rbuf, jbuf, abuf, t1, t2, t3,
+    kb0, kb1, kb2, kb3, vbuf, vstage, vtb, qbuf, idbuf, idsm, lens, pbuf, mq, lq, coef,
+    sq, gstat, obuf, mbuf, rbuf, jbuf, vjs, vjr, vjt, vjf, vjb, abuf, t1, t2, t3,
     local_sem, zsend, zrecv, ysend, yrecv, csend, crecv, qsend, qrecv, idsend, idrecv,
-    ssend, srecv, osend, orecv, asem, rsend, rrecv,
+    lsend, lrecv, jsend, jrecv, ssend, srecv, osend, orecv, asem, rsend, rrecv,
 ):
     n = lax.axis_index("ctx")
     g = lax.axis_index("resp")
@@ -82,9 +82,7 @@
     idload.start()
     qown = pltpu.make_async_copy(q_ref, qbuf.at[0], local_sem.at[2])
     qown.start()
-    jload = pltpu.make_async_copy(
-        judge_ref.at[pl.ds(pl.multiple_of(z * NY, NY), NY), :], jbuf, local_sem.at[3]
-    )
+    jload = pltpu.make_async_copy(judge_ref, jbuf, local_sem.at[3])
     jload.start()
 
     barrier = pltpu.get_barrier_semaphore()
@@ -94,11 +92,11 @@
         pl.semaphore_signal(barrier, inc=1, device_id=at_y((y + d) % NY), device_id_type=MESH)
     for d in range(1, NG):
         pl.semaphore_signal(barrier, inc=1, device_id=at_g((g + d) % NG), device_id_type=MESH)
-    vload.wait()
-    for j in range(NZ):
-        vtb[j] = jnp.transpose(vstage[:, j * HEAD:(j + 1) * HEAD]).reshape(2, POS, 128)
-    pltpu.make_async_copy(vtb.at[z, c], vbuf.at[z, half, quarter, c], zrecv.at[1, 0]).start()
-    idload.wait()
+    row = lax.broadcasted_iota(jnp.int32, (RESP, 128), 0)
+    lane = lax.broadcasted_iota(jnp.int32, (RESP, 128), 1)
+    own_lens = jnp.zeros((RESP, 128), jnp.int32)
+    for r in range(RESP):
+        own_lens = jnp.where(row == r, len_ref[r], own_lens)
     pl.semaphore_wait(barrier, NZ + NY + NG - 3)
 
     for d in (1, 7, 2, 6, 3, 5, 4):
@@ -107,16 +105,44 @@
             k_ref.at[krows, cols(zz)], kb0.at[z, half, c],
             zsend.at[0, d], zrecv.at[0, d], at_z(zz),
         )
+    for i in range(2):
+        for d in (1, 3):
+            part = pl.ds(4 * i if d == 1 else 4 - 4 * i, 4)
+            send(
+                q_ref.at[part], qbuf.at[4 - d, part], qsend.at[d, i], qrecv.at[4 - d, i], at_x(d)
+            )
+    vload.wait()
+    for j in range(NZ):
+        vtb[j] = jnp.transpose(vstage[:, j * HEAD:(j + 1) * HEAD]).reshape(2, POS, 128)
+    pltpu.make_async_copy(vtb.at[z, c], vbuf.at[z, half, quarter, c], zrecv.at[1, 0]).start()
     for d in (1, 7, 2, 6, 3, 5, 4):
         zz = (z + d) % NZ
         send(
             vtb.at[zz, c], vbuf.at[z, half, quarter, c],
             zsend.at[1, d], zrecv.at[1, d], at_z(zz),
         )
+    jload.wait()
+    for j in range(NZ):
+        rest = jbuf[j * NY:(j + 1) * NY, :]
+        terms = []
+        for _ in range(3):
+            terms.append(rest.astype(BF).astype(F32))
+            rest = rest - terms[-1]
+        terms.append(jnp.zeros((NY, HEAD), F32))
+        dots = jnp.dot(
+            jnp.concatenate(terms, axis=0).astype(BF), vtb[j].reshape(HEAD, 128),
+            preferred_element_type=F32,
+        )
+        vjs[j] = dots[:NY] + dots[NY:2 * NY] + dots[2 * NY:3 * NY]
+    vjr[z] = vjs[z]
+    for d in range(1, NZ):
+        zz = (z + d) % NZ
+        send(vjs.at[zz], vjr.at[z], jsend.at[0, d], jrecv.at[0, d], at_z(zz))
+    idload.wait()
+    lens[0] = own_lens * BLK
     for d in (1, 3, 2):
         send(idbuf.at[0], idbuf.at[4 - d], idsend.at[d], idrecv.at[4 - d], at_x(d))
-    for d in (1, 3):
-        send(q_ref, qbuf.at[4 - d], qsend.at[d], qrecv.at[4 - d], at_x(d))
+        send(lens.at[0], lens.at[4 - d], lsend.at[d], lrecv.at[4 - d], at_x(d))
 
     def chunk(w, j, zs, yy, cc):
         if w == 0:
@@ -156,8 +182,11 @@
                 to_next(w, way, 0, i)
             to_sibling(w, 0, 0, i)
 
-    def ring_step(w, t):
+    def ring_step(w, t, work=()):
+        work = list(work)
         for i in range(PIECES[w]):
+            if i % 2 == 0 and work:
+                work.pop(0)()
             for way in range(2):
                 if not valid(w, way, t, i):
                     continue
@@ -173,26 +202,53 @@
             arrived(piece(w, j, i, 1 - c), crecv.at[w, number, i])
 
     def forward_queries():
-        arrived(qbuf.at[1], qrecv.at[1])
-        send(
-            qbuf.at[1, pl.ds(4, 4)], qbuf.at[2, pl.ds(4, 4)], qsend.at[2], qrecv.at[2], at_x(3)
-        )
-        arrived(qbuf.at[3], qrecv.at[3])
-        send(
-            qbuf.at[3, pl.ds(0, 4)], qbuf.at[2, pl.ds(0, 4)], qsend.at[0], qrecv.at[0], at_x(1)
-        )
+        for d in (1, 3):
+            part = pl.ds(4 if d == 1 else 0, 4)
+            arrived(qbuf.at[d, part], qrecv.at[d, 0])
+            send(
+                qbuf.at[d, part], qbuf.at[2, part], qsend.at[2, d // 2], qrecv.at[2, d // 2],
+                at_x(4 - d),
+            )
 
     def wait_queries():
         qown.wait()
-        arrived(qbuf.at[2, pl.ds(4, 4)], qrecv.at[2])
-        arrived(qbuf.at[2, pl.ds(0, 4)], qrecv.at[0])
+        for d in (1, 3):
+            arrived(qbuf.at[d, pl.ds(0 if d == 1 else 4, 4)], qrecv.at[d, 1])
+            arrived(qbuf.at[2, pl.ds(4 if d == 1 else 0, 4)], qrecv.at[2, d // 2])
         for e in range(1, NX):
             arrived(idbuf.at[e], idrecv.at[e])
+            arrived(lens.at[e], lrecv.at[e])
         ids = pltpu.make_async_copy(idbuf, idsm, local_sem.at[1])
         ids.start()
         ids.wait()
 
-    def scores(j):
+    def judged_to_heads():
+        for d in range(1, NZ):
+            arrived(vjr.at[(z + NZ - d) % NZ], jrecv.at[0, d])
+        for yy in range(NY):
+            vjt[yy] = vjr[:, yy, :]
+        vjf[y] = vjt[y]
+        for d in range(1, NY):
+            yy = (y + d) % NY
+            send(vjt.at[yy], vjf.at[y], jsend.at[1, d], jrecv.at[1, d], at_y(yy))
+
+    def judged_values():
+        for d in range(1, NY):
+            arrived(vjf.at[(y + NY - d) % NY], jrecv.at[1, d])
+        line = lax.broadcasted_iota(jnp.int32, (16, 128), 0)
+
+        def one(zz, carry):
+            for yy in range(NY):
+                exact = jnp.broadcast_to(vjf[yy, pl.ds(zz, 1), :], (16, 128))
+                high = exact.astype(BF).astype(F32)
+                j = 2 * ((yy % 4 - quarter + 4) % 4)
+                tile = jnp.where(line == j, high, jnp.where(line == j + 1, exact - high, 0.0))
+                vjb[zz, yy // 4, yy % 4] = tile.astype(BF)
+            return carry
+
+        lax.fori_loop(0, NZ, one, 0)
+
+    def scores(j, part):
         def one(item, carry):
             e, r = item // RESP, item % RESP
             keys = []
@@ -210,47 +266,96 @@
             lq[j, e, pl.ds(r, 1), :] = jnp.sum(expo, axis=0, keepdims=True)
             return carry
 
-        lax.fori_loop(0, NX * RESP, one, 0, unroll=4)
+        lax.fori_loop(16 * part, 16 * part + 16, one, 0, unroll=8)
+
+    def both(j):
+        return [lambda: scores(j, 0), lambda: scores(j, 1)]
+
+    def spread(number, buf, own, size, where):
+        for d in range(1, size):
+            send(
+                buf.at[own], buf.at[own], rsend.at[number, d], rrecv.at[number, d],
+                where((own + d) % size),
+            )
+
+    def gather(number, buf, own, size):
+        for d in range(1, size):
+            arrived(buf.at[(own + size - d) % size], rrecv.at[number, d])
+
+    def probe(part):
+        def one(item, carry):
+            e, r = item // RESP, item % RESP
+            probes = []
+            for j in range(4):
+                for k in range(2):
+                    s = idsm[e, k, r]
+                    probes.append(vjb[s // 2, s % 2, (quarter + j) % 4])
+            dots = jnp.dot(
+                jnp.concatenate(probes, axis=1), pbuf[e, r].reshape(1024, TOK),
+                preferred_element_type=F32,
+            )
+            for j in range(4):
+                sq[j, e, pl.ds(r, 1), :] = dots[2 * j:2 * j + 1] + dots[2 * j + 1:2 * j + 2]
+            return carry
+
+        lax.fori_loop(16 * part, 16 * part + 16, one, 0, unroll=4)
 
     own_chunk(0)
+    forward_queries()
+    ring_step(0, 0)
+    judged_to_heads()
     own_chunk(1)
-    ring_step(0, 0)
-    forward_queries()
+    ring_step(0, 1)
+    wait_queries()
     ring_step(1, 0)
-    ring_step(0, 1)
-    ring_step(1, 1)
-    wait_queries()
     from_sibling(0, 2)
     from_sibling(0, 5)
-    scores(2)
-    ring_step(0, 2)
-    ring_step(1, 2)
+    ring_step(0, 2, both(2))
+    judged_values()
+    ring_step(1, 1)
     for number in (1, 3, 4, 6):
         from_sibling(0, number)
-    scores(1)
-    scores(3)
-    ring_step(0, 3)
-    ring_step(1, 3)
+    ring_step(0, 3, both(1))
+    scores(3, 0)
+    ring_step(1, 2, [lambda: scores(3, 1)])
     from_sibling(0, 0)
     from_sibling(0, 7)
-    scores(0)
-
-    row = lax.broadcasted_iota(jnp.int32, (RESP, 128), 0)
-    for e in (2, 1, 3, 0):
+    scores(0, 0)
+    scores(0, 1)
+
+    for e in range(NX):
         top = jnp.maximum(jnp.maximum(mq[0, e], mq[1, e]), jnp.maximum(mq[2, e], mq[3, e]))
-        scale = [jnp.exp2((mq[j, e] - top) * SCALE) for j in range(4)]
-        total = sum(scale[j] * lq[j, e] for j in range(4))
-        sstat[e, 0] = top
-        sstat[e, 1] = total
-        if e:
-            send(sstat.at[e], rstat.at[4 - e], ssend.at[e], srecv.at[4 - e], at_x(e))
-        if e == 2:
-            send(sstat.at[2], mstat.at[0], ssend.at[0], srecv.at[0], at_x(1))
-            send(sstat.at[2], mstat.at[1], ssend.at[4], srecv.at[4], at_x(3))
+        total = jnp.zeros((RESP, TOK), F32)
+        for j in range(4):
+            total = total + jnp.exp2((mq[j, e] - top) * SCALE) * lq[j, e]
+        gstat[x, (x + e) % NX, 0] = top
+        gstat[x, (x + e) % NX, 1] = total
+    for d in range(1, NX):
+        send(gstat.at[x], gstat.at[x], ssend.at[d], srecv.at[d], at_x(d))
+    probe(0)
+    ring_step(1, 3, [lambda: probe(1)])
+    for d in range(1, NX):
+        arrived(gstat.at[(x + NX - d) % NX], srecv.at[d])
+    for e in range(NX):
+        xx = (x + e) % NX
+        tops = [gstat[i, xx, 0] for i in range(NX)]
+        top = jnp.maximum(jnp.maximum(tops[0], tops[1]), jnp.maximum(tops[2], tops[3]))
+        total = jnp.zeros((RESP, TOK), F32)
+        for i in range(NX):
+            total = total + jnp.exp2((tops[i] - top) * SCALE) * gstat[i, xx, 1]
         inverse = 1.0 / total
         for j in range(4):
-            coef[e, j] = scale[j] * inverse
-    rstat[0] = sstat[0]
+            coef[e, j] = jnp.exp2((mq[j, e] - top) * SCALE) * inverse
+    judged = jnp.zeros((RESP, 128), F32)
+    for e in range(NX):
+        dots = jnp.zeros((RESP, 128), F32)
+        for j in range(4):
+            dots = dots + coef[e, j] * sq[j, e]
+        dots = jnp.sum(jnp.where(lane < lens[e], dots, 0.0), axis=1, keepdims=True)
+        dots = jnp.broadcast_to(dots, (RESP, 128)) / lens[e].astype(F32)
+        judged = judged + jnp.where(lane == (x + e) % NX, dots, 0.0)
+    t1[z] = judged
+    spread(0, t1, z, NZ, at_z)
     for number in range(8):
         from_sibling(1, number)
 
@@ -297,8 +402,8 @@
         first, second = output(1, r), output(3, 4 + r)
         arrived(mbuf.at[r], orecv.at[2, r])
         arrived(mbuf.at[4 + r], orecv.at[2, 4 + r])
-        first = first + mbuf[r].astype(F32) * wmerge[0, pl.ds(r, 1), :]
-        second = second + mbuf[4 + r].astype(F32) * wmerge[1, pl.ds(4 + r, 1), :]
+        first = first + mbuf[r].astype(F32)
+        second = second + mbuf[4 + r].astype(F32)
         obuf[1, r] = first.astype(BF)
         obuf[3, 4 + r] = second.astype(BF)
         out_copy(1, r).start()
@@ -311,85 +416,48 @@
         rbuf[0, 4 + r] = second.astype(BF)
         return carry
 
-    lax.fori_loop(0, 4, opposite, 0)
-    lax.fori_loop(0, 4, beside, 0)
-    arrived(mstat.at[0], srecv.at[0])
-    arrived(mstat.at[1], srecv.at[4])
-    for i, e in ((0, 1), (1, 3)):
-        top = jnp.maximum(sstat[e, 0], mstat[i, 0])
-        here = jnp.exp2((sstat[e, 0] - top) * SCALE) * sstat[e, 1]
-        there = jnp.exp2((mstat[i, 0] - top) * SCALE) * mstat[i, 1]
-        inverse = 1.0 / (here + there)
-        wmerge[i] = there * inverse
-        here = jnp.where((row < 4) == (i == 0), here * inverse, 1.0)
-        for j in range(4):
-            coef[e, j] = coef[e, j] * here
-    lax.fori_loop(0, 4, merged, 0)
-    lax.fori_loop(0, 4, mine, 0)
-
-    for e in range(1, NX):
-        arrived(rstat.at[e], srecv.at[e])
-    tops = rstat[:, 0]
-    weight = jnp.exp2((tops - jnp.max(tops, axis=0, keepdims=True)) * SCALE) * rstat[:, 1]
-    weight = weight / jnp.sum(weight, axis=0, keepdims=True)
-    rstat[0, 0] = weight[0]
-    rstat[1, 0] = weight[1] + jnp.where(row < 4, 0.0, weight[2])
-    rstat[3, 0] = weight[3] + jnp.where(row < 4, weight[2], 0.0)
-    jload.wait()
-    judge = jnp.transpose(jnp.broadcast_to(jbuf[pl.ds(y, 1), :], (TOK, HEAD)))
+    lax.fori_loop(0, 4, opposite, 0, unroll=2)
+    lax.fori_loop(0, 4, beside, 0, unroll=2)
+    gather(0, t1, z, NZ)
+    t2[y] = jnp.sum(t1[...], axis=0)
+    spread(1, t2, y, NY, at_y)
+    lax.fori_loop(0, 4, mine, 0, unroll=2)
+    lax.fori_loop(0, 4, merged, 0, unroll=2)
+    gather(1, t2, y, NY)
+    t3[g] = jnp.sum(t2[...], axis=0)
+    spread(2, t3, g, NG, at_g)
+
     token = lax.broadcasted_iota(jnp.int32, (HEAD, TOK), 1)
 
     def att_copy(r):
         return pltpu.make_async_copy(abuf.at[r], att_ref.at[r], asem.at[r])
 
     def combine(r):
-        total = rstat[0, 0, pl.ds(r, 1), :] * rbuf[0, r].astype(F32)
+        total = rbuf[0, r].astype(F32)
         for e in (1, 3):
             arrived(rbuf.at[e, r], orecv.at[e, r])
-            total = total + rstat[e, 0, pl.ds(r, 1), :] * rbuf[e, r].astype(F32)
+            total = total + rbuf[e, r].astype(F32)
         total = jnp.where(token < BLK * len_ref[r], total, 0.0).astype(BF)
         abuf[r] = jnp.transpose(total)
         att_copy(r).start()
-        t1[z, pl.ds(r, 1), :] = jnp.sum(total.astype(F32) * judge, axis=0, keepdims=True)
 
     def combine_pair(r, carry):
         combine(r)
         combine(4 + r)
         return carry
 
+    drain()
     lax.fori_loop(0, 4, combine_pair, 0)
-
-    def spread(number, buf, own, size, where):
-        copies = []
-        for d in range(1, size):
-            copy = remote(
-                buf.at[own], buf.at[own], rsend.at[number, d], rrecv.at[number, d],
-                where((own + d) % size),
-            )
-            copy.start()
-            copies.append(copy)
-        drain()
-        sent.extend(copies)
-        for d in range(1, size):
-            arrived(buf.at[(own + size - d) % size], rrecv.at[number, d])
-
-    spread(0, t1, z, NZ, at_z)
-    t2[y] = jnp.sum(t1[...], axis=0)
-    spread(1, t2, y, NY, at_y)
-    dots = jnp.sum(jnp.sum(t2[...], axis=0), axis=1, keepdims=True)
-    lane = lax.broadcasted_iota(jnp.int32, (RESP, 128), 1)
-    tokens = jnp.ones((RESP, 128), F32)
-    for r in range(RESP):
-        tokens = jnp.where(row == r, (BLK * len_ref[r]).astype(F32), tokens)
-    t3[g] = jnp.broadcast_to(dots, (RESP, 128)) / tokens
-    spread(2, t3, g, NG, at_g)
+    gather(2, t3, g, NG)
     flat = jnp.zeros((RESP, 128), F32)
-    for i in range(NG):
-        flat = flat + jnp.where(lane == i * RESP + row, t3[i], 0.0)
+    for i in range(NC):
+        scored = t3[i] + t3[2 + i] + t3[4 + i] + t3[6 + i]
+        for xx in range(NX):
+            column = jnp.broadcast_to(scored[:, xx:xx + 1], (RESP, 128))
+            flat = flat + jnp.where(lane == (xx * NC + i) * RESP + row, column, 0.0)
     flat = jnp.sum(flat, axis=0, keepdims=True)
     flat = flat - jnp.sum(flat, axis=1, keepdims=True) / (NG * RESP)
     rel_ref[...] = flat[:, :NG * RESP]
-    drain()
 
     def finish(r, carry):
         for copy in out_copy(2, r):
@@ -427,18 +495,22 @@
             pltpu.VMEM((NX, RESP, TOK, HEAD), BF),
             pltpu.VMEM((NX, 2, RESP), jnp.int32),
             pltpu.SMEM((NX, 2, RESP), jnp.int32),
+            pltpu.VMEM((NX, RESP, 128), jnp.int32),
             pltpu.VMEM((NX, RESP, 4, 256, TOK), BF),
             pltpu.VMEM((4, NX, RESP, TOK), F32),
             pltpu.VMEM((4, NX, RESP, TOK), F32),
             pltpu.VMEM((NX, 4, RESP, TOK), F32),
-            pltpu.VMEM((2, RESP, TOK), F32),
-            pltpu.VMEM((NX, 2, RESP, TOK), F32),
-            pltpu.VMEM((NX, 2, RESP, TOK), F32),
-            pltpu.VMEM((2, 2, RESP, TOK), F32),
+            pltpu.VMEM((4, NX, RESP, TOK), F32),
+            pltpu.VMEM((NX, NX, 2, RESP, TOK), F32),
             pltpu.VMEM((NX, RESP, HEAD, TOK), BF),
             pltpu.VMEM((RESP, HEAD, TOK), BF),
             pltpu.VMEM((NX, RESP, HEAD, TOK), BF),
-            pltpu.VMEM((NY, HEAD), F32),
+            pltpu.VMEM((NZ * NY, HEAD), F32),
+            pltpu.VMEM((NZ, NY, 128), F32),
+            pltpu.VMEM((NZ, NY, 128), F32),
+            pltpu.VMEM((NY, NZ, 128), F32),
+            pltpu.VMEM((NY, NZ, 128), F32),
+            pltpu.VMEM((NZ, 2, 4, 16, 128), BF),
             pltpu.VMEM((RESP, TOK, HEAD), BF),
             pltpu.VMEM((NZ, RESP, TOK), F32),
             pltpu.VMEM((NY, RESP, TOK), F32),
@@ -450,12 +522,16 @@
             dma((2, 2, 4, 4)),
             dma((2, 8, 4)),
             dma((2, 8, 4)),
+            dma((NX, 2)),
+            dma((NX, 2)),
             dma((NX,)),
             dma((NX,)),
             dma((NX,)),
             dma((NX,)),
-            dma((5,)),
-            dma((5,)),
+            dma((2, 8)),
+            dma((2, 8)),
+            dma((NX,)),
+            dma((NX,)),
             dma((NX, RESP)),
             dma((NX, RESP)),
             dma((RESP,)),

time: 81.5 us -> 69.7 us (0.86)
  Pallas kernels: 78.5 us -> 66.7 us
    pallas_call x1, Pallas kernels: 78.5 us -> 66.7 us  [local(): pl.pallas_call(kernel, out_shape=(jax.ShapeDtypeStruct((RESP, TOK, HEAD),...]
where the time goes in v3:
time: 69.7 us; the launch traced here: 69.5 us
  Pallas kernels  66.7 us (96%)
  local copies, waits for them, and re-layouts  2.19 us (3%)
    pallas_call x1, Pallas kernels, local(): pl.pallas_call(kernel, out_shape=(jax.ShapeDtypeStruct((RESP, TOK, HEAD),...  66.7 us
    unnamed x4, local copies, waits for them, and re-layouts  2.19 us

profile of v3, /device:TPU:1, one launch (start us, length us, event | category | flops | bytes accessed | tf_op | source)
XLA Modules:
  0.0 69.5 jit_solution(9775584442409893693)
XLA Ops:
  0.6 66.7 %shard_map.77 = (bf16[8,128,128]{2,1,0:T(8,128)(2,1)}, f32[1,64]{1,0:T(1,128)}) custom-call(bf16[8,128,128]{2,1,0:T(8,128)(2,1)} %q_ref.1, bf16[512,1024]{1,0:T(8,128)(2,1)} %k_ref.1, bf16[512,1024]{1,0:T(8,128)(2,1)} %v_ref.1, s32[2,8]{1,0:T(2,128)} %bitcast.4, s32[8]{0:T(128)} %len_ref.1, f32[64,128]{1,0:T(8,128)} %bitcast.3), custom_call_target="tpu_custom_call" | custom-call | tf_op jit(solution)/shard_map/pallas_call | solution.py:479
  67.3 0.0 copy-start
  67.3 1.7 %copy.10 = bf16[8,128,128]{2,1,0:T(8,128)(2,1)} copy(bf16[8,128,128]{2,1,0:T(8,128)(2,1)} %get-tuple-element.8) | data formatting | bytes 524288
  69.0 0.0 copy-done
  69.0 0.5 copy.11
Async XLA Ops:
  67.3 1.7 %copy-start = (f32[1,64]{1,0:T(1,128)S(1)}, f32[1,64]{1,0:T(1,128)}, u32[]{:S(2)}) copy-start(f32[1,64]{1,0:T(1,128)} %get-tuple-element.5) | copy-start | bytes 772

commit v4 on v3

--- a/solution.py
+++ b/solution.py
@@ -15,7 +15,7 @@
 RESP = 8
 BLK = 64
 POS = 64
-PIECES = (4, 4)
+PIECES = (4, 2)
 SCALE = math.log2(math.e) / math.sqrt(HEAD)
 BF = jnp.bfloat16
 F32 = jnp.float32
@@ -26,8 +26,7 @@
     att_ref, rel_ref,
     kb0, kb1, kb2, kb3, vbuf, vstage, vtb, qbuf, idbuf, idsm, lens, pbuf, mq, lq, coef,
     sq, gstat, obuf, mbuf, rbuf, jbuf, vjs, vjr, vjt, vjf, vjb, abuf, t1, t2, t3,
-    local_sem, zsend, zrecv, ysend, yrecv, csend, crecv, qsend, qrecv, idsend, idrecv,
-    lsend, lrecv, jsend, jrecv, ssend, srecv, osend, orecv, asem, rsend, rrecv,
+    local_sem, sent_sem, zrecv, yrecv, crecv, qrecv, idrecv, jrecv, srecv, orecv, rrecv,
 ):
     n = lax.axis_index("ctx")
     g = lax.axis_index("resp")
@@ -55,19 +54,19 @@
             src_ref=src, dst_ref=dst, send_sem=ss, recv_sem=rs, device_id=dev, device_id_type=MESH
         )
 
-    sent = []
-
-    def send(src, dst, ss, rs, dev):
-        copy = remote(src, dst, ss, rs, dev)
-        copy.start()
-        sent.append(copy)
+    def send(src, dst, kind, rs, dev):
+        remote(src, dst, sent_sem.at[kind], rs, dev).start()
 
     def arrived(dst, rs):
         remote(dst, dst, rs, rs, sibling).wait_recv()
 
-    def drain():
-        while sent:
-            sent.pop(0).wait_send()
+    def all_sent(ref, kind):
+        remote(ref, ref, sent_sem.at[kind], sent_sem.at[kind], sibling).wait_send()
+
+    def block(w, zz):
+        count = PIECES[w]
+        width = NZ // count
+        return (z // width + count - zz // width) % count
 
     rows = pl.ds(pl.multiple_of(x * 128, 128), 128)
     krows = pl.ds(pl.multiple_of(x * 128 + c * POS, POS), POS)
@@ -103,13 +102,13 @@
         zz = (z + d) % NZ
         send(
             k_ref.at[krows, cols(zz)], kb0.at[z, half, c],
-            zsend.at[0, d], zrecv.at[0, d], at_z(zz),
+            0, zrecv.at[0, block(0, zz)], at_z(zz),
         )
     for i in range(2):
         for d in (1, 3):
             part = pl.ds(4 * i if d == 1 else 4 - 4 * i, 4)
             send(
-                q_ref.at[part], qbuf.at[4 - d, part], qsend.at[d, i], qrecv.at[4 - d, i], at_x(d)
+                q_ref.at[part], qbuf.at[4 - d, part], 3, qrecv.at[4 - d, i], at_x(d)
             )
     vload.wait()
     for j in range(NZ):
@@ -119,30 +118,13 @@
         zz = (z + d) % NZ
         send(
             vtb.at[zz, c], vbuf.at[z, half, quarter, c],
-            zsend.at[1, d], zrecv.at[1, d], at_z(zz),
+            0, zrecv.at[1, block(1, zz)], at_z(zz),
         )
-    jload.wait()
-    for j in range(NZ):
-        rest = jbuf[j * NY:(j + 1) * NY, :]
-        terms = []
-        for _ in range(3):
-            terms.append(rest.astype(BF).astype(F32))
-            rest = rest - terms[-1]
-        terms.append(jnp.zeros((NY, HEAD), F32))
-        dots = jnp.dot(
-            jnp.concatenate(terms, axis=0).astype(BF), vtb[j].reshape(HEAD, 128),
-            preferred_element_type=F32,
-        )
-        vjs[j] = dots[:NY] + dots[NY:2 * NY] + dots[2 * NY:3 * NY]
-    vjr[z] = vjs[z]
-    for d in range(1, NZ):
-        zz = (z + d) % NZ
-        send(vjs.at[zz], vjr.at[z], jsend.at[0, d], jrecv.at[0, d], at_z(zz))
     idload.wait()
     lens[0] = own_lens * BLK
     for d in (1, 3, 2):
-        send(idbuf.at[0], idbuf.at[4 - d], idsend.at[d], idrecv.at[4 - d], at_x(d))
-        send(lens.at[0], lens.at[4 - d], lsend.at[d], lrecv.at[4 - d], at_x(d))
+        send(idbuf.at[0], idbuf.at[4 - d], 4, idrecv.at[0], at_x(d))
+        send(lens.at[0], lens.at[4 - d], 5, idrecv.at[1], at_x(d))
 
     def chunk(w, j, zs, yy, cc):
         if w == 0:
@@ -157,6 +139,12 @@
 
     def valid(w, way, t, i):
         return t < 3 or (i < PIECES[w] // 2) == (way == 0)
+
+    def hop(w, way, t, i):
+        count = PIECES[w]
+        size = 3 * count + count // 2
+        step = t * count + i if t < 3 else 3 * count + i % (count // 2)
+        return (7 * PIECES[0] if w else 0) + way * size + step
 
     def to_next(w, way, t, i):
         j = -t if way == 0 else t
@@ -165,22 +153,18 @@
         first = ((z // width + i) % count) * width
         dst = chunk(w, j + (-1 if way == 0 else 1), pl.ds(first, width), (y + j + NY) % NY, c)
         dev = at_y((y + (1 if way == 0 else NY - 1)) % NY)
-        send(piece(w, j, i, c), dst, ysend.at[w, way, t, i], yrecv.at[w, way, t, i], dev)
-
-    def to_sibling(w, number, j, i):
+        send(piece(w, j, i, c), dst, 1, yrecv.at[hop(w, way, t, i)], dev)
+
+    def to_sibling(w, j, i):
         ref = piece(w, j, i, c)
-        send(ref, ref, csend.at[w, number, i], crecv.at[w, number, i], sibling)
+        send(ref, ref, 2, crecv.at[4 if w else j % 4], sibling)
 
     def own_chunk(w):
-        count = PIECES[w]
-        width = NZ // count
-        for i in range(count):
-            for k in range(width):
-                zz = ((z // width + i) % count) * width + k
-                arrived(chunk(w, 0, zz, y, c), zrecv.at[w, (z + NZ - zz) % NZ])
+        for i in range(PIECES[w]):
+            arrived(piece(w, 0, i, c), zrecv.at[w, i])
             for way in range(2):
                 to_next(w, way, 0, i)
-            to_sibling(w, 0, 0, i)
+            to_sibling(w, 0, i)
 
     def ring_step(w, t, work=()):
         work = list(work)
@@ -191,22 +175,20 @@
                 if not valid(w, way, t, i):
                     continue
                 j = -1 - t if way == 0 else 1 + t
-                arrived(piece(w, j, i, c), yrecv.at[w, way, t, i])
+                arrived(piece(w, j, i, c), yrecv.at[hop(w, way, t, i)])
                 if t < 3 and valid(w, way, t + 1, i):
                     to_next(w, way, t + 1, i)
-                to_sibling(w, (1 + 3 * way + t) if t < 3 else 7, j, i)
-
-    def from_sibling(w, number):
-        j = (0, -1, -2, -3, 1, 2, 3, 4)[number]
-        for i in range(PIECES[w]):
-            arrived(piece(w, j, i, 1 - c), crecv.at[w, number, i])
+                to_sibling(w, j, i)
+
+    def from_sibling(j):
+        arrived(kb[j].at[:, :, 1 - c], crecv.at[j])
 
     def forward_queries():
         for d in (1, 3):
             part = pl.ds(4 if d == 1 else 0, 4)
             arrived(qbuf.at[d, part], qrecv.at[d, 0])
             send(
-                qbuf.at[d, part], qbuf.at[2, part], qsend.at[2, d // 2], qrecv.at[2, d // 2],
+                qbuf.at[d, part], qbuf.at[2, part], 3, qrecv.at[2, d // 2],
                 at_x(4 - d),
             )
 
@@ -215,26 +197,42 @@
         for d in (1, 3):
             arrived(qbuf.at[d, pl.ds(0 if d == 1 else 4, 4)], qrecv.at[d, 1])
             arrived(qbuf.at[2, pl.ds(4 if d == 1 else 0, 4)], qrecv.at[2, d // 2])
-        for e in range(1, NX):
-            arrived(idbuf.at[e], idrecv.at[e])
-            arrived(lens.at[e], lrecv.at[e])
+        arrived(idbuf.at[pl.ds(0, 3)], idrecv.at[0])
+        arrived(lens.at[pl.ds(0, 3)], idrecv.at[1])
         ids = pltpu.make_async_copy(idbuf, idsm, local_sem.at[1])
         ids.start()
         ids.wait()
 
+    def judge_values():
+        jload.wait()
+        for j in range(NZ):
+            rest = jbuf[j * NY:(j + 1) * NY, :]
+            terms = []
+            for _ in range(3):
+                terms.append(rest.astype(BF).astype(F32))
+                rest = rest - terms[-1]
+            terms.append(jnp.zeros((NY, HEAD), F32))
+            dots = jnp.dot(
+                jnp.concatenate(terms, axis=0).astype(BF), vtb[j].reshape(HEAD, 128),
+                preferred_element_type=F32,
+            )
+            vjs[j] = dots[:NY] + dots[NY:2 * NY] + dots[2 * NY:3 * NY]
+        vjr[z] = vjs[z]
+        for d in range(1, NZ):
+            zz = (z + d) % NZ
+            send(vjs.at[zz], vjr.at[z], 6, jrecv.at[0], at_z(zz))
+
     def judged_to_heads():
-        for d in range(1, NZ):
-            arrived(vjr.at[(z + NZ - d) % NZ], jrecv.at[0, d])
+        arrived(vjr.at[pl.ds(0, NZ - 1)], jrecv.at[0])
         for yy in range(NY):
             vjt[yy] = vjr[:, yy, :]
         vjf[y] = vjt[y]
         for d in range(1, NY):
             yy = (y + d) % NY
-            send(vjt.at[yy], vjf.at[y], jsend.at[1, d], jrecv.at[1, d], at_y(yy))
+            send(vjt.at[yy], vjf.at[y], 7, jrecv.at[1], at_y(yy))
 
     def judged_values():
-        for d in range(1, NY):
-            arrived(vjf.at[(y + NY - d) % NY], jrecv.at[1, d])
+        arrived(vjf.at[pl.ds(0, NY - 1)], jrecv.at[1])
         line = lax.broadcasted_iota(jnp.int32, (16, 128), 0)
 
         def one(zz, carry):
@@ -274,13 +272,11 @@
     def spread(number, buf, own, size, where):
         for d in range(1, size):
             send(
-                buf.at[own], buf.at[own], rsend.at[number, d], rrecv.at[number, d],
-                where((own + d) % size),
-            )
-
-    def gather(number, buf, own, size):
-        for d in range(1, size):
-            arrived(buf.at[(own + size - d) % size], rrecv.at[number, d])
+                buf.at[own], buf.at[own], 9 + number, rrecv.at[number], where((own + d) % size)
+            )
+
+    def gather(number, buf):
+        arrived(buf.at[pl.ds(0, 7)], rrecv.at[number])
 
     def probe(part):
         def one(item, carry):
@@ -303,23 +299,21 @@
     own_chunk(0)
     forward_queries()
     ring_step(0, 0)
-    judged_to_heads()
+    judge_values()
     own_chunk(1)
     ring_step(0, 1)
     wait_queries()
     ring_step(1, 0)
-    from_sibling(0, 2)
-    from_sibling(0, 5)
+    from_sibling(2)
     ring_step(0, 2, both(2))
-    judged_values()
+    judged_to_heads()
     ring_step(1, 1)
-    for number in (1, 3, 4, 6):
-        from_sibling(0, number)
+    from_sibling(1)
+    from_sibling(3)
     ring_step(0, 3, both(1))
     scores(3, 0)
     ring_step(1, 2, [lambda: scores(3, 1)])
-    from_sibling(0, 0)
-    from_sibling(0, 7)
+    from_sibling(0)
     scores(0, 0)
     scores(0, 1)
 
@@ -331,11 +325,11 @@
         gstat[x, (x + e) % NX, 0] = top
         gstat[x, (x + e) % NX, 1] = total
     for d in range(1, NX):
-        send(gstat.at[x], gstat.at[x], ssend.at[d], srecv.at[d], at_x(d))
+        send(gstat.at[x], gstat.at[x], 8, srecv.at[0], at_x(d))
+    judged_values()
     probe(0)
     ring_step(1, 3, [lambda: probe(1)])
-    for d in range(1, NX):
-        arrived(gstat.at[(x + NX - d) % NX], srecv.at[d])
+    arrived(gstat.at[pl.ds(0, 3)], srecv.at[0])
     for e in range(NX):
         xx = (x + e) % NX
         tops = [gstat[i, xx, 0] for i in range(NX)]
@@ -356,8 +350,7 @@
         judged = judged + jnp.where(lane == (x + e) % NX, dots, 0.0)
     t1[z] = judged
     spread(0, t1, z, NZ, at_z)
-    for number in range(8):
-        from_sibling(1, number)
+    arrived(vbuf.at[:, :, :, 1 - c], crecv.at[4])
 
     def output(e, r):
         out = jnp.zeros((HEAD, TOK), F32)
@@ -372,42 +365,37 @@
             out = out + part * coef[e, j, pl.ds(r, 1), :]
         return out
 
-    def out_copy(e, r):
+    def out_send(e, r):
         if e == 2:
-            return [
-                remote(
-                    obuf.at[2, rr], mbuf.at[rr], osend.at[2, rr], orecv.at[2, rr], at_x(d)
-                )
-                for rr, d in ((r, 1), (4 + r, 3))
-            ]
-        return remote(obuf.at[e, r], rbuf.at[4 - e, r], osend.at[e, r], orecv.at[4 - e, r], at_x(e))
+            send(obuf.at[2, r], mbuf.at[r], 12, orecv.at[r], at_x(1))
+            send(obuf.at[2, 4 + r], mbuf.at[4 + r], 12, orecv.at[r], at_x(3))
+        else:
+            send(obuf.at[e, r], rbuf.at[4 - e, r], 12, orecv.at[4 + r % 4], at_x(e))
 
     def opposite(r, carry):
         first, second = output(2, r), output(2, 4 + r)
         obuf[2, r] = first.astype(BF)
         obuf[2, 4 + r] = second.astype(BF)
-        for copy in out_copy(2, r):
-            copy.start()
+        out_send(2, r)
         return carry
 
     def beside(r, carry):
         first, second = output(1, 4 + r), output(3, r)
         obuf[1, 4 + r] = first.astype(BF)
         obuf[3, r] = second.astype(BF)
-        out_copy(1, 4 + r).start()
-        out_copy(3, r).start()
+        out_send(1, 4 + r)
+        out_send(3, r)
         return carry
 
     def merged(r, carry):
         first, second = output(1, r), output(3, 4 + r)
-        arrived(mbuf.at[r], orecv.at[2, r])
-        arrived(mbuf.at[4 + r], orecv.at[2, 4 + r])
+        arrived(mbuf.at[pl.ds(0, 2)], orecv.at[r])
         first = first + mbuf[r].astype(F32)
         second = second + mbuf[4 + r].astype(F32)
         obuf[1, r] = first.astype(BF)
         obuf[3, 4 + r] = second.astype(BF)
-        out_copy(1, r).start()
-        out_copy(3, 4 + r).start()
+        out_send(1, r)
+        out_send(3, 4 + r)
         return carry
 
     def mine(r, carry):
@@ -418,37 +406,40 @@
 
     lax.fori_loop(0, 4, opposite, 0, unroll=2)
     lax.fori_loop(0, 4, beside, 0, unroll=2)
-    gather(0, t1, z, NZ)
+    gather(0, t1)
     t2[y] = jnp.sum(t1[...], axis=0)
     spread(1, t2, y, NY, at_y)
     lax.fori_loop(0, 4, mine, 0, unroll=2)
     lax.fori_loop(0, 4, merged, 0, unroll=2)
-    gather(1, t2, y, NY)
+    gather(1, t2)
     t3[g] = jnp.sum(t2[...], axis=0)
     spread(2, t3, g, NG, at_g)
 
     token = lax.broadcasted_iota(jnp.int32, (HEAD, TOK), 1)
-
-    def att_copy(r):
-        return pltpu.make_async_copy(abuf.at[r], att_ref.at[r], asem.at[r])
 
     def combine(r):
         total = rbuf[0, r].astype(F32)
         for e in (1, 3):
-            arrived(rbuf.at[e, r], orecv.at[e, r])
             total = total + rbuf[e, r].astype(F32)
         total = jnp.where(token < BLK * len_ref[r], total, 0.0).astype(BF)
         abuf[r] = jnp.transpose(total)
-        att_copy(r).start()
+        pltpu.make_async_copy(abuf.at[r], att_ref.at[r], local_sem.at[4]).start()
 
     def combine_pair(r, carry):
+        arrived(rbuf.at[pl.ds(0, 2), pl.ds(0, 2)], orecv.at[4 + r])
         combine(r)
         combine(4 + r)
         return carry
 
-    drain()
+    for ref, kind in (
+        (vtb.at[pl.ds(0, 7)], 0), (vbuf.at[pl.ds(0, 7)], 1), (vbuf, 2), (qbuf.at[pl.ds(0, 3)], 3),
+        (idbuf.at[pl.ds(0, 3)], 4), (lens.at[pl.ds(0, 3)], 5), (vjs.at[pl.ds(0, 7)], 6),
+        (vjt.at[pl.ds(0, 7)], 7), (gstat.at[pl.ds(0, 3)], 8), (t1.at[pl.ds(0, 7)], 9),
+        (t2.at[pl.ds(0, 7)], 10),
+    ):
+        all_sent(ref, kind)
     lax.fori_loop(0, 4, combine_pair, 0)
-    gather(2, t3, g, NG)
+    gather(2, t3)
     flat = jnp.zeros((RESP, 128), F32)
     for i in range(NC):
         scored = t3[i] + t3[2 + i] + t3[4 + i] + t3[6 + i]
@@ -458,17 +449,9 @@
     flat = jnp.sum(flat, axis=0, keepdims=True)
     flat = flat - jnp.sum(flat, axis=1, keepdims=True) / (NG * RESP)
     rel_ref[...] = flat[:, :NG * RESP]
-
-    def finish(r, carry):
-        for copy in out_copy(2, r):
-            copy.wait_send()
-        for rr in (r, 4 + r):
-            out_copy(1, rr).wait_send()
-            out_copy(3, rr).wait_send()
-            att_copy(rr).wait()
-        return carry
-
-    lax.fori_loop(0, 4, finish, 0)
+    all_sent(t3.at[pl.ds(0, 7)], 11)
+    all_sent(obuf.at[pl.ds(1, 3)], 12)
+    pltpu.make_async_copy(abuf, att_ref, local_sem.at[4]).wait()
 
 
 def local(queries, keys, values, span_ids, lengths, judge):
@@ -515,28 +498,17 @@
             pltpu.VMEM((NZ, RESP, TOK), F32),
             pltpu.VMEM((NY, RESP, TOK), F32),
             pltpu.VMEM((NG, RESP, TOK), F32),
-            dma((4,)),
-            dma((2, NZ)),
-            dma((2, NZ)),
-            dma((2, 2, 4, 4)),
-            dma((2, 2, 4, 4)),
-            dma((2, 8, 4)),
-            dma((2, 8, 4)),
+            dma((5,)),
+            dma((13,)),
+            dma((2, 4)),
+            dma((7 * (PIECES[0] + PIECES[1]),)),
+            dma((5,)),
             dma((NX, 2)),
-            dma((NX, 2)),
-            dma((NX,)),
-            dma((NX,)),
-            dma((NX,)),
-            dma((NX,)),
-            dma((2, 8)),
-            dma((2, 8)),
-            dma((NX,)),
-            dma((NX,)),
-            dma((NX, RESP)),
-            dma((NX, RESP)),
-            dma((RESP,)),
-            dma((3, 8)),
-            dma((3, 8)),
+            dma((2,)),
+            dma((2,)),
+            dma((1,)),
+            dma((8,)),
+            dma((3,)),
         ],
         compiler_params=pltpu.CompilerParams(
             collective_id=0, has_side_effects=True, vmem_limit_bytes=60 * 1024 * 1024

time: 69.7 us -> 65.8 us (0.944)
  Pallas kernels: 66.7 us -> 62.8 us
    pallas_call x1, Pallas kernels: 66.7 us -> 62.8 us  [local(): pl.pallas_call(kernel, out_shape=(jax.ShapeDtypeStruct((RESP, TOK, HEAD),...]
where the time goes in v4:
time: 65.8 us; the launch traced here: 65.6 us
  Pallas kernels  62.8 us (95%)
  local copies, waits for them, and re-layouts  2.19 us (3%)
    pallas_call x1, Pallas kernels, local(): pl.pallas_call(kernel, out_shape=(jax.ShapeDtypeStruct((RESP, TOK, HEAD),...  62.8 us
    unnamed x4, local copies, waits for them, and re-layouts  2.19 us

profile of v4, /device:TPU:1, one launch (start us, length us, event | category | flops | bytes accessed | tf_op | source)
XLA Modules:
  0.0 65.6 jit_solution(8597841568326167193)
XLA Ops:
  0.6 62.8 %shard_map.77 = (bf16[8,128,128]{2,1,0:T(8,128)(2,1)}, f32[1,64]{1,0:T(1,128)}) custom-call(bf16[8,128,128]{2,1,0:T(8,128)(2,1)} %q_ref.1, bf16[512,1024]{1,0:T(8,128)(2,1)} %k_ref.1, bf16[512,1024]{1,0:T(8,128)(2,1)} %v_ref.1, s32[2,8]{1,0:T(2,128)} %bitcast.4, s32[8]{0:T(128)} %len_ref.1, f32[64,128]{1,0:T(8,128)} %bitcast.3), custom_call_target="tpu_custom_call" | custom-call | tf_op jit(solution)/shard_map/pallas_call | solution.py:462
  63.4 0.0 copy-start
  63.5 1.7 %copy.10 = bf16[8,128,128]{2,1,0:T(8,128)(2,1)} copy(bf16[8,128,128]{2,1,0:T(8,128)(2,1)} %get-tuple-element.8) | data formatting | bytes 524288
  65.1 0.0 copy-done
  65.1 0.5 copy.11
Async XLA Ops:
  63.4 1.7 %copy-start = (f32[1,64]{1,0:T(1,128)S(1)}, f32[1,64]{1,0:T(1,128)}, u32[]{:S(2)}) copy-start(f32[1,64]{1,0:T(1,128)} %get-tuple-element.5) | copy-start | bytes 772
